TPU v7x, 256 devices: a whole 4x4x8 slice. The times are simulated.
256 devices in a mesh: dp: 64 (over z, y, core), seq: 4 (over x).
Axes of the slice: x: 4, y: 4, z: 8, core: 2. Of those that a mesh axis runs over, the one named last changes fastest.
Arguments:
- queries: bfloat16 [64, 512, 1024], P('dp', 'seq'), may hold values from -6 to 6
- key_rows: bfloat16 [64, 512, 1024], P('dp', 'seq'), may hold values from -6 to 6
- value_rows: bfloat16 [64, 512, 1024], P('dp', 'seq'), may hold values from -6 to 6
- inputs: bfloat16 [64, 512, 1024], P('dp', 'seq'), may hold values from -6 to 6
- w_gate: float32 [1024, 32], replicated, may hold values from -0.1875 to 0.1875
- poly_coef: float32 [1024], replicated, may hold values from -0.6 to 0.6
- decay_rate: float32 [16], replicated, may hold values from 0.0003 to 0.05
- cotangent: bfloat16 [64, 512, 1024], P('dp', 'seq'), may hold values from -6 to 6
Outputs:
- grad_queries: bfloat16 [64, 512, 1024], P('dp', 'seq')
- grad_keys: bfloat16 [64, 512, 1024], P('dp', 'seq')
- grad_values: bfloat16 [64, 512, 1024], P('dp', 'seq')
- grad_inputs: bfloat16 [64, 512, 1024], P('dp', 'seq')
- grad_gate: float32 [1024, 32], replicated
- grad_coef: float32 [1024], replicated
- grad_rate: float32 [16], replicated
All inputs are finite; a program needn't handle non-finite values.
Results may differ from a plain program's by a relative error of at most 0.02.
Values may be sent and summed in bfloat16 or wider, within the bound.
A program may use at most 64 MiB of HBM per device.

v0:
```python
import jax
import jax.numpy as jnp
from jax import lax
from jax.sharding import PartitionSpec as P

WINDOW = 64


highest = lax.Precision.HIGHEST


def passed_along(value, axis, steps):
    count = lax.axis_size(axis)
    first, last = (max(0, -steps), min(count, count - steps))
    return lax.ppermute(value, axis, [(source, source + steps) for source in range(first, last)])


def prefix(x, axis, join, neutral):
    place = lax.axis_index(axis)
    gathered = jax.tree.map(
        lambda a, kind: lax.all_gather(a.astype(kind), axis), x, (jnp.bfloat16, jnp.bfloat16)
    )
    state = jax.tree.map(lambda a, e: jnp.zeros_like(a) + jnp.asarray(e, a.dtype), x, neutral)

    def one(hop, state):
        return join(
            state,
            jax.tree.map(
                lambda a, own: lax.dynamic_index_in_dim(a, hop, 0, False).astype(own.dtype),
                gathered,
                x,
            ),
        )

    return lax.fori_loop(0, place, one, state)


def entering(x, axis, combine, identity):
    count, index = (lax.axis_size(axis), lax.axis_index(axis))
    everything = jax.tree.map(
        lambda part, kind: lax.all_gather(part.astype(kind), axis),
        x,
        jax.tree.map(lambda a: jnp.bfloat16 if a.dtype == jnp.float32 else a.dtype, x),
    )
    start = jax.tree.map(
        lambda part, zero: jnp.broadcast_to(jnp.asarray(zero, part.dtype), part.shape), x, identity
    )

    def hop(k, before):
        at = count - 1 - k
        reached = at > index
        new = combine(
            before, jax.tree.map(lambda part, own: part[at].astype(own.dtype), everything, x)
        )
        return jax.tree.map(lambda a, b: jnp.where(reached, a, b), new, before)

    return lax.fori_loop(0, count, hop, start)


def features(raw, poly_coef):
    as_float = raw.astype(jnp.float32)
    return 0.125 * (as_float + poly_coef * as_float * as_float)


def window_table(window):
    step_ids = lax.broadcasted_iota(jnp.int32, (window, 2 * window), 0)
    slot_ids = lax.broadcasted_iota(jnp.int32, (window, 2 * window), 1)
    offset = step_ids - slot_ids + window
    return ((offset >= 0) & (offset < window)).astype(jnp.float32)


def block_step(memory, block_in):
    q_block, key_pairs, value_pairs, decay_log = block_in
    window = q_block.shape[0]
    head_count = decay_log.shape[1]
    head_dim = q_block.shape[1] // head_count
    log_decay = jnp.cumsum(decay_log, axis=0)
    row_ids = lax.broadcasted_iota(jnp.int32, (window, window), 0)
    col_ids = lax.broadcasted_iota(jnp.int32, (window, window), 1)
    causal = col_ids <= row_ids
    gap_log = jnp.where(causal[:, :, None], log_decay[:, None, :] - log_decay[None, :, :], 0.0)
    decay_mat = jnp.where(causal[:, :, None], jnp.exp(gap_log), 0.0)
    window_mask = window_table(window)
    kernel = jnp.einsum("tsh,si->hti", decay_mat, window_mask, precision=highest)
    q_heads = q_block.reshape(window, head_count, head_dim)
    key_heads = key_pairs.reshape(2 * window, head_count, head_dim)
    value_heads = value_pairs.reshape(2 * window, head_count, head_dim)
    scores = jnp.einsum("thd,ihd->hti", q_heads, key_heads, preferred_element_type=jnp.float32)
    weights = (scores * kernel).astype(jnp.bfloat16)
    inside = jnp.einsum("hti,ihd->thd", weights, value_heads, preferred_element_type=jnp.float32)
    carried_out = (
        jnp.einsum("thd,hde->the", q_heads.astype(jnp.float32), memory, precision=highest)
        * jnp.exp(log_decay)[:, :, None]
    )
    last_row = kernel[:, window - 1, :]
    carried = (key_heads.astype(jnp.float32) * jnp.transpose(last_row)[:, :, None]).astype(
        jnp.bfloat16
    )
    update = jnp.einsum("ihd,ihe->hde", carried, value_heads, preferred_element_type=jnp.float32)
    memory_next = jnp.exp(log_decay[window - 1])[:, None, None] * memory + update
    return (memory_next, (inside + carried_out).reshape(window, head_count * head_dim))


def state_step(memory, block_in):
    key_pairs, value_pairs, decay_log = block_in
    window = decay_log.shape[0]
    head_count = decay_log.shape[1]
    head_dim = key_pairs.shape[1] // head_count
    log_decay = jnp.cumsum(decay_log, axis=0)
    tail_decay = jnp.exp(log_decay[window - 1][None, :] - log_decay)
    last_row = jnp.einsum("sh,si->hi", tail_decay, window_table(window), precision=highest)
    key_heads = key_pairs.reshape(2 * window, head_count, head_dim)
    value_heads = value_pairs.reshape(2 * window, head_count, head_dim)
    carried = (key_heads.astype(jnp.float32) * jnp.transpose(last_row)[:, :, None]).astype(
        jnp.bfloat16
    )
    update = jnp.einsum("ihd,ihe->hde", carried, value_heads, preferred_element_type=jnp.float32)
    return (jnp.exp(log_decay[window - 1])[:, None, None] * memory + update, None)


def prepare(
    key_rows, value_rows, inputs, w_gate, poly_coef, decay_rate, key_rim, value_rim, input_rim
):
    length = key_rows.shape[0]
    window = key_rim.shape[0]
    head_count = decay_rate.shape[0]
    width_all = key_rows.shape[1]
    head_dim = width_all // head_count
    blocks = length // window
    all_inputs = jnp.concatenate([input_rim, inputs], axis=0)
    logits = jnp.dot(all_inputs.astype(jnp.float32), w_gate, precision=highest)
    decay_log = -decay_rate * jax.nn.softplus(logits[window:, :head_count])
    gamma = jax.nn.sigmoid(logits[:, head_count:]) / window
    all_keys = jnp.concatenate([key_rim, key_rows], axis=0)
    all_values = jnp.concatenate([value_rim, value_rows], axis=0)
    weighted = (
        (features(all_keys, poly_coef).reshape(-1, head_count, head_dim) * gamma[:, :, None])
        .astype(jnp.bfloat16)
        .reshape(-1, width_all)
    )
    key_pairs = jnp.concatenate(
        [
            weighted[:length].reshape(blocks, window, width_all),
            weighted[window:].reshape(blocks, window, width_all),
        ],
        axis=1,
    )
    value_pairs = jnp.concatenate(
        [
            all_values[:length].reshape(blocks, window, width_all),
            all_values[window:].reshape(blocks, window, width_all),
        ],
        axis=1,
    )
    return (key_pairs, value_pairs, decay_log)


def state_pass(
    key_rows, value_rows, inputs, w_gate, poly_coef, decay_rate, key_rim, value_rim, input_rim
):
    key_pairs, value_pairs, decay_log = prepare(
        key_rows, value_rows, inputs, w_gate, poly_coef, decay_rate, key_rim, value_rim, input_rim
    )
    window = key_rim.shape[0]
    head_count = decay_rate.shape[0]
    head_dim = key_rows.shape[1] // head_count
    blocks = key_rows.shape[0] // window
    start = jnp.zeros((head_count, head_dim, head_dim), jnp.float32)
    memory_end = lax.scan(
        state_step, start, (key_pairs, value_pairs, decay_log.reshape(blocks, window, head_count))
    )[0]
    return (memory_end, jnp.sum(decay_log, axis=0))


def local_forward(
    queries,
    key_rows,
    value_rows,
    inputs,
    w_gate,
    poly_coef,
    decay_rate,
    key_rim,
    value_rim,
    input_rim,
    memory,
):
    length = queries.shape[0]
    window = key_rim.shape[0]
    head_count = decay_rate.shape[0]
    width_all = queries.shape[1]
    blocks = length // window
    key_pairs, value_pairs, decay_log = prepare(
        key_rows, value_rows, inputs, w_gate, poly_coef, decay_rate, key_rim, value_rim, input_rim
    )
    query_feat = features(queries, poly_coef).astype(jnp.bfloat16)
    memory_end, outputs = lax.scan(
        block_step,
        memory,
        (
            query_feat.reshape(blocks, window, width_all),
            key_pairs,
            value_pairs,
            decay_log.reshape(blocks, window, head_count),
        ),
    )
    return (outputs.reshape(length, width_all), memory_end, jnp.sum(decay_log, axis=0))


def compose(earlier, later):
    return (later[0] * earlier[0], later[0][:, None, None] * earlier[1] + later[1])


def on_device(queries, key_rows, value_rows, inputs, w_gate, poly_coef, decay_rate, cotangent):
    own_queries = queries[0]
    own_keys = key_rows[0]
    own_values = value_rows[0]
    own_inputs = inputs[0]
    rim_parts = passed_along(
        (own_keys[-WINDOW:], own_values[-WINDOW:], own_inputs[-WINDOW:]), "seq", 1
    )
    operands = (
        own_queries,
        own_keys,
        own_values,
        own_inputs,
        w_gate,
        poly_coef,
        decay_rate,
        rim_parts[0],
        rim_parts[1],
        rim_parts[2],
    )
    partial_memory, decay_total = state_pass(
        own_keys,
        own_values,
        own_inputs,
        w_gate,
        poly_coef,
        decay_rate,
        rim_parts[0],
        rim_parts[1],
        rim_parts[2],
    )
    factor = jnp.exp(decay_total)
    identity = (jnp.ones_like(factor), jnp.zeros_like(partial_memory))
    memory_in = prefix((factor, partial_memory), "seq", compose, identity)[1]
    primal, pullback = jax.vjp(local_forward, *operands, memory_in)
    upstream = cotangent[0].astype(jnp.float32)
    local_adjoint = pullback((upstream, jnp.zeros_like(primal[1]), jnp.zeros_like(primal[2])))[10]
    memory_grad = entering((factor, local_adjoint), "seq", compose, identity)[1]
    grads = pullback((upstream, memory_grad, jnp.zeros_like(primal[2])))
    returned = passed_along((grads[7], grads[8], grads[9]), "seq", -1)
    grad_keys = jnp.concatenate([grads[1][:-WINDOW], grads[1][-WINDOW:] + returned[0]], axis=0)
    grad_values = jnp.concatenate([grads[2][:-WINDOW], grads[2][-WINDOW:] + returned[1]], axis=0)
    grad_inputs = jnp.concatenate([grads[3][:-WINDOW], grads[3][-WINDOW:] + returned[2]], axis=0)
    totals = lax.psum((grads[4], grads[5], grads[6]), ("dp", "seq"))
    return (
        grads[0][None],
        grad_keys[None],
        grad_values[None],
        grad_inputs[None],
        totals[0],
        totals[1],
        totals[2],
    )


def solution(mesh):
    placed = (
        P("dp", "seq", None),
        P("dp", "seq", None),
        P("dp", "seq", None),
        P("dp", "seq", None),
        P(),
        P(),
        P(),
        P("dp", "seq", None),
    )
    return jax.shard_map(
        on_device,
        mesh=mesh,
        in_specs=placed,
        out_specs=(
            P("dp", "seq", None),
            P("dp", "seq", None),
            P("dp", "seq", None),
            P("dp", "seq", None),
            P(),
            P(),
            P(),
        ),
        check_vma=False,
    )
```

profile of v0, /device:TPU:1, one launch (start us, length us, event | category | flops | bytes accessed | tf_op | source)
XLA Modules:
  0.0 436.7 jit_solution(8241140920143847961)
XLA Ops:
  7.2 1.0 slice_bitcast_fusion.4
  8.2 4.1 collective-permute-start
  12.4 3.1 collective-permute-start.1
  16.2 3.5 collective-permute-start.2
  19.6 1.7 fusion.130
  32.1 1.0 copy.181
  33.1 3.2 while.130
  33.4 1.0 constant_dynamic-slice_fusion.32
  35.0 1.0 constant_dynamic-slice_fusion.32
  36.4 11.3 %all-gather.1 = bf16[64,64,64]{2,1,0:T(8,128)(2,1)S(1)} all-gather(bf16[16,64,64]{2,1,0:T(8,128)(2,1)S(1)} %convert_element_type.327), channel_id=3, replica_groups=mesh['dp'=64,'seq'=4] {'seq'}, dimensions={0}, use_global_device_ids=true | all-gather | bytes 655360 | tf_op jit(solution)/shard_map/all_gather | solution.py:21
  47.9 6.9 %all-reduce.8 = bf16[64]{0:T(256)(128)(2,1)S(1)} all-reduce(bf16[64]{0:T(256)(128)(2,1)S(1)} %dynamic-update-slice), channel_id=2, replica_groups=mesh['dp'=64,'seq'=4] {'seq'}, use_global_device_ids=true, to_apply=%add.8 | all-reduce | flops 64 | bytes 256
  55.7 32.4 %while.128 = (s32[]{:T(128)}, f32[16,64,64]{2,1,0:T(8,128)S(1)}, f32[2,64,64,16]{2,3,1,0:T(8,128)}, bf16[2,128,16,64]{1,3,2,0:T(8,128)(2,1)}, bf16[2,64,16,64]{3...) while((s32[]{:T(128)}, f32[16,64,64]{2,1,0:T(8,128)S(1)}, ...), condition=%wide.region_8.9_spmd.clone.clone, body=%wide.region_6.8_spmd.clone.clone.sunk | while | flops 186301440 | bytes 31898088 | solution.py:197
  55.9 1.5 bitcast_dynamic-update-slice_fusion.12
  58.5 1.0 bitcast_dynamic-update-slice_fusion.13
  59.9 1.2 constant_dynamic-slice_fusion.24
  62.1 1.2 fusion.216
  65.6 1.0 copy-done.52
  66.6 1.3 dynamic_update_slice.252
  72.1 1.5 bitcast_dynamic-update-slice_fusion.12
  74.7 1.0 bitcast_dynamic-update-slice_fusion.13
  76.1 1.2 constant_dynamic-slice_fusion.24
  78.3 1.2 fusion.216
  81.8 1.0 copy-done.52
  82.8 1.3 dynamic_update_slice.252
  89.0 7.9 %while.131 = (s32[]{:T(128)}, f32[16,64,64]{2,1,0:T(8,128)}, f32[2,16,1,1]{1,3,2,0:T(1,128)S(1)}, f32[2,64,16,64]{1,3,2,0:T(8,128)}, f32[2,64,1024]{2,1,0:T(8,12...) while((s32[]{:T(128)}, f32[16,64,64]{2,1,0:T(8,128)}, ...), condition=%wide.region_10.11_spmd.clone, body=%wide.region_9.10_spmd.clone.sunk | while | flops 50593796 | bytes 4469107 | solution.py:197
  90.1 2.0 convolution_add_fusion.11
  94.1 2.0 convolution_add_fusion.11
  96.9 1.1 convert_element_type.334
  98.0 12.0 %all-gather.2 = bf16[64,64,64]{2,1,0:T(8,128)(2,1)S(1)} all-gather(bf16[16,64,64]{2,1,0:T(8,128)(2,1)S(1)} %convert_element_type.334), channel_id=4, replica_groups=mesh['dp'=64,'seq'=4] {'seq'}, dimensions={0}, use_global_device_ids=true | all-gather | bytes 655360 | tf_op jit(solution)/shard_map/all_gather | solution.py:41
  113.2 57.0 %while.129 = (s32[]{:T(128)}, f32[16,64,64]{2,1,0:T(8,128)S(1)}, bf16[2,64,1024]{2,1,0:T(8,128)(2,1)}, bf16[2,128,1024]{2,1,0:T(8,128)(2,1)}, bf16[2,128,1024]{1...) while((s32[]{:T(128)}, f32[16,64,64]{2,1,0:T(8,128)S(1)}, ...), condition=%wide.region_20.21_spmd.clone.clone, body=%wide.region_13.20_spmd.clone.clone.sunk | while | flops 304790528 | bytes 45722872 | solution.py:197
  114.1 1.2 fusion.233
  115.3 1.4 fusion.235
  116.7 1.2 fusion.239
  119.1 1.1 constant_dynamic-slice_fusion.28
  121.4 1.3 fusion.241
  124.5 2.2 convolution_convert_fusion.9
  126.8 1.0 copy-done.19
  129.1 1.6 constant_dynamic-update-slice_fusion.19
  130.7 1.0 constant_dynamic-slice_fusion.30
  131.6 1.0 copy.303
  133.3 1.2 fusion.236
  138.5 2.0 convolution_add_fusion.9
  142.6 1.2 fusion.233
  143.8 1.4 fusion.235
  145.2 1.2 fusion.239
  146.6 0.9 fusion.240
  147.6 1.1 constant_dynamic-slice_fusion.28
  149.9 1.3 fusion.241
  153.0 2.2 convolution_convert_fusion.9
  155.3 1.0 copy-done.19
  157.6 1.6 constant_dynamic-update-slice_fusion.19
  159.2 1.0 constant_dynamic-slice_fusion.30
  160.2 1.0 copy.303
  161.8 1.2 fusion.236
  167.0 2.0 convolution_add_fusion.9
  170.9 1.1 fusion.154
  176.6 1.0 fusion.135
  178.4 1.3 collective-permute-start.5
  181.1 1.3 collective-permute-start.4
  182.8 1.4 collective-permute-start.3
  184.4 90.7 %all-reduce.9 = (f32[1024]{0:T(1024)}, f32[16]{0:T(128)}) all-reduce(f32[1024]{0:T(1024)S(1)} %add_any.125, f32[16]{0:T(128)S(1)} %neg.24), channel_id=1, replica_groups=mesh['dp'=64,'seq'=4] {'dp','seq'}, use_global_device_ids=true, to_apply=%region_25.26 | all-reduce | flops 1040 | bytes 8320 | tf_op jit(solution)/shard_map/psum | solution.py:257
  276.9 0.9 fusion.138
  280.2 148.0 %all-reduce.12.cloned.1.call-done = f32[1024,32]{0,1:T(8,128)} async-done(((f32[1024,32]{0,1:T(8,128)}), f32[1024,32]{0,1:T(8,128)}) %all-reduce.12.cloned.1.call-update) | async-done | bytes 131088 | tf_op jit(solution)/shard_map/psum | solution.py:257
  428.3 1.6 copy.434
  (380 shorter events, 74.4 us)
Async XLA Ops:
  7.2 18.2 %copy-start = (f32[1024,32]{0,1:T(8,128)S(1)}, f32[1024,32]{0,1:T(8,128)}, u32[]{:S(2)}) copy-start(f32[1024,32]{0,1:T(8,128)} %param.24) | copy-start | bytes 393220
  7.2 5.1 %copy-start.28 = (bf16[1,128,1024]{2,1,0:T(8,128)(2,1)S(1)}, bf16[1,128,1024]{2,1,0:T(8,128)(2,1)}, u32[]{:S(2)}) copy-start(bf16[1,128,1024]{2,1,0:T(8,128)(2,1)} %param.21) | copy-start | bytes 786436
  7.2 8.3 %copy-start.27 = (bf16[1,128,1024]{2,1,0:T(8,128)(2,1)S(1)}, bf16[1,128,1024]{2,1,0:T(8,128)(2,1)}, u32[]{:S(2)}) copy-start(bf16[1,128,1024]{2,1,0:T(8,128)(2,1)} %param.22) | copy-start | bytes 786436
  7.2 421.1 %all-reduce.12.cloned.1.call-start = ((), (), s32[]{:S(2)}) async-start(), calls=%async_computation | async-start | bytes 262144 | tf_op jit(solution)/shard_map/psum | solution.py:257
  8.2 11.4 %copy-start.31 = (bf16[1,128,1024]{2,1,0:T(8,128)(2,1)S(1)}, bf16[1,128,1024]{2,1,0:T(8,128)(2,1)}, u32[]{:S(2)}) copy-start(bf16[1,128,1024]{2,1,0:T(8,128)(2,1)} %param.20) | copy-start | bytes 786436
  8.2 17.1 %collective-permute-start = (bf16[64,1024]{1,0:T(8,128)(2,1)S(1)}, bf16[64,1024]{1,0:T(8,128)(2,1)S(1)}, u32[]{:S(2)}, u32[]{:S(2)}) collective-permute-start(bf16[64,1024]{1,0:T(8,128)(2,1)S(1)} %slice_bitcast_fusion.4), channel_id=1, source_target_pairs={{0,1},{1,2},{2,3},{4,5},{5,6},{6,7},{8,9},{9,10},{10,11},{12,13},{... | collective-permute-start | bytes 393224 | tf_op jit(solution)/shard_map/ppermute | solution.py:15
  12.4 14.2 %collective-permute-start.1 = (bf16[64,1024]{1,0:T(8,128)(2,1)S(1)}, bf16[64,1024]{1,0:T(8,128)(2,1)S(1)}, u32[]{:S(2)}, u32[]{:S(2)}) collective-permute-start(bf16[64,1024]{1,0:T(8,128)(2,1)S(1)} %slice_bitcast_fusion.3), channel_id=1, source_target_pairs={{0,1},{1,2},{2,3},{4,5},{5,6},{6,7},{8,9},{9,10},{10,11},{12,13},{... | collective-permute-start | bytes 393224 | tf_op jit(solution)/shard_map/ppermute | solution.py:15
  16.2 14.9 %collective-permute-start.2 = (bf16[64,1024]{1,0:T(8,128)(2,1)}, bf16[64,1024]{1,0:T(8,128)(2,1)}, u32[]{:S(2)}, u32[]{:S(2)}) collective-permute-start(bf16[64,1024]{1,0:T(8,128)(2,1)} %slice_bitcast_fusion.2), channel_id=1, source_target_pairs={{0,1},{1,2},{2,3},{4,5},{5,6},{6,7},{8,9},{9,10},{10,11},{12,13},{... | collective-permute-start | bytes 393224 | tf_op jit(solution)/shard_map/ppermute | solution.py:15
  21.3 2.1 copy-start.38
  22.0 5.3 %copy-start.20 = (bf16[1,128,1024]{1,2,0:T(8,128)(2,1)}, bf16[1,128,1024]{1,2,0:T(8,128)(2,1)S(1)}, u32[]{:S(2)}) copy-start(bf16[1,128,1024]{1,2,0:T(8,128)(2,1)S(1)} %copy.176) | copy-start | bytes 786436
  23.4 2.0 copy-start.47
  58.5 1.0 copy-start.14
  59.6 1.6 copy-start.17
  59.9 1.2 copy-start.15
  59.9 1.3 copy-start.9
  62.1 1.2 copy-start.10
  62.1 1.2 copy-start.18
  64.2 1.2 copy-start.51
  65.4 2.5 copy-start.33
  65.6 1.0 copy-start.52
  69.8 1.2 copy-start.12
  74.7 1.0 copy-start.14
  75.8 1.6 copy-start.17
  76.1 1.2 copy-start.15
  76.1 1.3 copy-start.9
  78.3 1.2 copy-start.10
  78.3 1.2 copy-start.18
  80.4 1.2 copy-start.51
  81.6 2.5 copy-start.33
  81.8 1.0 copy-start.52
  86.0 1.2 copy-start.12
  89.1 1.0 copy-start.3
  93.0 1.0 copy-start.3
  116.7 1.4 copy-start.53
  124.4 2.3 copy-start.5
  124.5 2.2 copy-start.39
  126.7 1.0 copy-start.19
  134.6 1.0 copy-start.25
  134.6 1.9 copy-start.16
  136.5 1.0 copy-start.11
  138.5 2.1 copy-start.6
  138.5 2.9 copy-start.40
  140.5 1.2 copy-start.2
  145.2 1.4 copy-start.53
  153.0 2.3 copy-start.5
  153.0 2.2 copy-start.39
  155.2 1.0 copy-start.19
  163.1 1.0 copy-start.25
  163.1 1.9 copy-start.16
  165.0 1.0 copy-start.11
  167.0 2.1 copy-start.6
  167.0 2.9 copy-start.40
  169.0 1.2 copy-start.2
  172.1 1.0 copy-start.23
  176.6 3.0 copy-start.8
  178.4 97.6 %collective-permute-start.5 = (bf16[64,1024]{1,0:T(8,128)(2,1)}, bf16[64,1024]{1,0:T(8,128)(2,1)}, u32[]{:S(2)}, u32[]{:S(2)}) collective-permute-start(bf16[64,1024]{1,0:T(8,128)(2,1)} %get-tuple-element.1970), channel_id=1, source_target_pairs={{1,0},{2,1},{3,2},{5,4},{6,5},{7,6},{9,8},{10,9},{11,10},{13,12},{... | collective-permute-start | bytes 393224 | tf_op jit(solution)/shard_map/ppermute | solution.py:15
  180.3 2.1 copy-start.29
  180.3 2.1 copy-start.36
  180.3 2.1 copy-start.46
  181.1 95.8 %collective-permute-start.4 = (bf16[64,1024]{1,0:T(8,128)(2,1)}, bf16[64,1024]{1,0:T(8,128)(2,1)}, u32[]{:S(2)}, u32[]{:S(2)}) collective-permute-start(bf16[64,1024]{1,0:T(8,128)(2,1)} %get-tuple-element.1962), channel_id=1, source_target_pairs={{1,0},{2,1},{3,2},{5,4},{6,5},{7,6},{9,8},{10,9},{11,10},{13,12},{... | collective-permute-start | bytes 393224 | tf_op jit(solution)/shard_map/ppermute | solution.py:15
  182.4 1.8 copy-start.30
  182.8 1.5 copy-start.24
  182.8 96.7 %collective-permute-start.3 = (bf16[64,1024]{1,0:T(8,128)(2,1)S(1)}, bf16[64,1024]{1,0:T(8,128)(2,1)S(1)}, u32[]{:S(2)}, u32[]{:S(2)}) collective-permute-start(bf16[64,1024]{1,0:T(8,128)(2,1)S(1)} %get-tuple-element.1972), channel_id=1, source_target_pairs={{1,0},{2,1},{3,2},{5,4},{6,5},{7,6},{9,8},{10,9},{11,10},{13,12},{... | collective-permute-start | bytes 393224 | tf_op jit(solution)/shard_map/ppermute | solution.py:15
  184.2 90.9 %copy-start.32 = (bf16[1,128,1024]{2,1,0:T(8,128)(2,1)S(1)}, bf16[1,128,1024]{2,1,0:T(8,128)(2,1)}, u32[]{:S(2)}) copy-start(bf16[1,128,1024]{2,1,0:T(8,128)(2,1)} %param.20) | copy-start | bytes 786436
  (33 other events, 24.7 us)
Sparse Core Ops, SparseCore 0:
  177.8 250.4 all-reduce.11
where the time goes:
time: 440 us; the launch traced here: 437 us
  waiting for transfers between devices  148 us (34%)
  blocking collectives  121 us (28%)
  local copies, waits for them, and re-layouts  73.8 us (17%)
  matrix products  35.3 us (8%)
  other arithmetic  27.4 us (6%)
  between operations  15.4 us (4%)
  starting transfers between devices  14.7 us (3%)
    psum x1, waiting for transfers between devices, on_device(): totals = lax.psum((grads[4], grads[5], grads[6]), ('dp', 'seq'))  148 us
    psum x1, blocking collectives, on_device(): totals = lax.psum((grads[4], grads[5], grads[6]), ('dp', 'seq'))  90.7 us
    while x116, local copies, waits for them, and re-layouts  20.7 us
    dot_general x8, matrix products, block_step(): jnp.einsum('thd,hde->the', q_heads.astype(jnp.float32), memory, precision...  15 us
    ppermute x6, starting transfers between devices, passed_along(): lax.ppermute(value, axis, [(source, source + steps) for source in range(f...  14.7 us
    dynamic_update_slice x28, local copies, waits for them, and re-layouts, local_forward(): lax.scan(block_step, memory, (query_feat.reshape(blocks, window, width_al...  12.6 us
    all_gather x1, blocking collectives, entering(): lax.all_gather(part.astype(kind), axis)  12 us
    unnamed x73, local copies, waits for them, and re-layouts  11.6 us
  transfers between devices with their start and end apart: 7, of which 1 were waited for; matrix products, arithmetic and copies ran while one was open for 3% of the time, Pallas kernels for 0%

commit v1 on v0

v1 whole, which is shorter than its diff:
```python
import functools

import jax
import jax.numpy as jnp
from jax import lax
from jax.experimental import pallas as pl
from jax.experimental.pallas import tpu as pltpu
from jax.sharding import PartitionSpec as P

BLOCK = 64
LANES = 128
WIDTH = 1024
PAIRS = WIDTH // LANES
HEADS = 16
F32 = jnp.float32
BF16 = jnp.bfloat16
MESH = pl.DeviceIdType.MESH


def nn(a, b):
    return lax.dot_general(a, b, (((1,), (0,)), ((), ())), preferred_element_type=F32)


def nt(a, b):
    return lax.dot_general(a, b, (((1,), (1,)), ((), ())), preferred_element_type=F32)


def tn(a, b):
    return lax.dot_general(a, b, (((0,), (0,)), ((), ())), preferred_element_type=F32)


def pieces(a, count):
    parts = []
    for _ in range(count):
        part = a.astype(BF16)
        parts.append(part)
        a = a - part.astype(F32)
    return parts


def flag(condition):
    return jnp.where(condition, 1.0, 0.0).astype(BF16)


def iota(shape, dimension):
    return lax.broadcasted_iota(jnp.int32, shape, dimension)


Q_UP, G_UP, L_UP, S_UP, SS2_UP, SS3_UP, TOT1, TOT2, TOT3 = range(9)
P_DN, R_DN, T2_DN, T3_DN, DQ_DN, DA_DN = range(9, 15)
MESSAGES = 15


def main_kernel(
    q_ref, k_ref, v_ref, x_ref, w_ref, coef_ref, rate_ref, g_ref,
    dq_ref, dk_ref, dv_ref, dx_ref, part_ref,
    qn, gn, lbuf, tot, tot_in, s1_out, ss_out, s1_in, ss_in, p_out, r_out, t_out, p_in, r_in, t_in,
    dqn_out, dqn_in, dan_out, dan_in,
    lrow, lx, gamma_x, blast_x, qf, wk, gq, s0c, u0c, c1c, m_in, m_mid, n_mid, n_end, z_end,
    dqf, dwk, dvf, gmat, xmat,
    send_sem, recv_sem,
):
    place = lax.axis_index("seq")
    last = 3

    def copy(source, target, message, to):
        return pltpu.make_async_remote_copy(
            src_ref=source,
            dst_ref=target,
            send_sem=send_sem.at[message],
            recv_sem=recv_sem.at[message],
            device_id={"seq": to},
            device_id_type=MESH,
        )

    up1, up2, up3 = place - 1, place - 2, place - 3
    dn1, dn2, dn3 = place + 1, place + 2, place + 3
    around = [lax.rem(place + 4 - hop, 4) for hop in (1, 2, 3)]
    copies = {
        Q_UP: (copy(q_ref.at[pl.ds(0, BLOCK)], qn, Q_UP, up1), 1),
        G_UP: (copy(g_ref.at[pl.ds(0, BLOCK)], gn, G_UP, up1), 1),
        L_UP: (copy(lbuf.at[pl.ds(0, BLOCK)], lbuf.at[pl.ds(2 * BLOCK, BLOCK)], L_UP, up1), 1),
        S_UP: (copy(s1_out, s1_in, S_UP, up1), 1),
        SS2_UP: (copy(ss_out, ss_in.at[0], SS2_UP, up2), 2),
        SS3_UP: (copy(ss_out, ss_in.at[1], SS3_UP, up3), 3),
        TOT1: (copy(tot, tot_in.at[0], TOT1, around[0]), 0),
        TOT2: (copy(tot, tot_in.at[1], TOT2, around[1]), 0),
        TOT3: (copy(tot, tot_in.at[2], TOT3, around[2]), 0),
        P_DN: (copy(p_out, p_in, P_DN, dn1), -1),
        R_DN: (copy(r_out, r_in, R_DN, dn1), -1),
        T2_DN: (copy(t_out, t_in.at[0], T2_DN, dn2), -2),
        T3_DN: (copy(t_out, t_in.at[1], T3_DN, dn3), -3),
        DQ_DN: (copy(dqn_out, dqn_in, DQ_DN, dn1), -1),
        DA_DN: (copy(dan_out, dan_in, DA_DN, dn1), -1),
    }

    def guarded(steps, action):
        if steps == 0:
            action()
        elif steps > 0:
            pl.when(place >= steps)(action)
        else:
            pl.when(place <= last + steps)(action)

    def send(message):
        description, steps = copies[message]
        guarded(steps, description.start)

    def sent(message):
        description, steps = copies[message]
        guarded(steps, description.wait_send)

    def received(message):
        description, steps = copies[message]
        guarded(-steps, description.wait_recv)

    barrier = pltpu.get_barrier_semaphore()
    for hop in (1, 2, 3):
        pl.semaphore_signal(
            barrier, inc=1, device_id={"seq": lax.rem(place + hop, 4)}, device_id_type=MESH
        )

    @pl.when(place == last)
    def _():
        qn[...] = jnp.zeros_like(qn)
        gn[...] = jnp.zeros_like(gn)
        lbuf[pl.ds(2 * BLOCK, BLOCK), :] = jnp.zeros((BLOCK, LANES), F32)
        s1_in[...] = jnp.zeros_like(s1_in)

    for hop in (2, 3):
        @pl.when(place > last - hop)
        def _():
            ss_in[hop - 2] = jnp.zeros(ss_in.shape[1:], BF16)

        @pl.when(place < hop)
        def _():
            t_in[hop - 2] = jnp.zeros(t_in.shape[1:], BF16)

    @pl.when(place == 0)
    def _():
        p_in[...] = jnp.zeros_like(p_in)
        r_in[...] = jnp.zeros_like(r_in)
        dqn_in[...] = jnp.zeros_like(dqn_in)
        dan_in[...] = jnp.zeros_like(dan_in)

    w_hi, w_lo = pieces(
        jnp.concatenate([w_ref[...], jnp.zeros((LANES - 2 * HEADS, WIDTH), F32)], axis=0), 2
    )
    pl.semaphore_wait(barrier, 3)
    send(Q_UP)
    send(G_UP)
    x = x_ref[...]
    logits = nt(x, w_hi) + nt(x, w_lo)
    small = jnp.exp(-jnp.abs(logits))
    soft = jnp.maximum(logits, 0.0) + jnp.log1p(small)
    sig = jnp.where(logits >= 0.0, 1.0, small) / (1.0 + small)
    rate = jnp.concatenate([rate_ref[...], jnp.zeros((1, LANES - HEADS), F32)], axis=1)
    decay = -rate * soft
    gamma = sig * (1.0 / BLOCK)
    row, col = iota((LANES, LANES), 0), iota((LANES, LANES), 1)
    same = (row // BLOCK) == (col // BLOCK)
    tri = flag(same & (col <= row))
    log_own = sum(nn(tri, part) for part in pieces(decay, 3))
    lbuf[pl.ds(0, LANES), :] = log_own
    tot[...] = jnp.zeros_like(tot)
    tot[0:1, :] = log_own[BLOCK - 1 : BLOCK]
    tot[1:2, :] = log_own[LANES - 1 :]
    send(L_UP)
    for message in (TOT1, TOT2, TOT3):
        send(message)

    head_row = iota((LANES, WIDTH), 0)
    head_lane = iota((LANES, WIDTH), 1) // BLOCK
    spread = flag(head_row == head_lane)
    spread_gate = flag(head_row == head_lane + HEADS)
    left = iota((BLOCK, LANES), 1) < BLOCK
    left1 = iota((1, LANES), 1) < BLOCK

    def expand(a, count):
        return sum(nn(part, spread) for part in pieces(a, count))

    def block_rows(logs, block, offset):
        pick = flag(row == (col % BLOCK) + offset)
        turned = sum(tn(part, pick) for part in pieces(logs, 3))
        for pair in range(PAIRS):
            lrow[block : block + 1, pl.ds(pair * LANES, LANES)] = jnp.where(
                left1, turned[2 * pair : 2 * pair + 1], turned[2 * pair + 1 : 2 * pair + 2]
            )

    block_rows(log_own, 0, 0)
    block_rows(log_own, 1, BLOCK)
    lx[pl.ds(0, LANES), :] = expand(log_own, 3)
    gamma_x[...] = sum(nn(part, spread_gate) for part in pieces(gamma, 2))

    srow, scol = iota((BLOCK, BLOCK), 0), iota((BLOCK, BLOCK), 1)
    cur_t = flag(scol >= srow)
    prev_t = flag(scol < srow)
    tail0 = jnp.exp(log_own[BLOCK - 1 : BLOCK] - log_own[:BLOCK])
    tail1 = jnp.exp(log_own[LANES - 1 :] - log_own[BLOCK:])

    def ending(mask, tail):
        return expand(sum(nn(mask, part) for part in pieces(tail, 2)), 2)

    blast_x[pl.ds(0, BLOCK), :] = ending(cur_t, tail0)
    blast_x[pl.ds(BLOCK, BLOCK), :] = ending(prev_t, tail1)
    blast_x[pl.ds(2 * BLOCK, BLOCK), :] = ending(cur_t, tail1)

    def lanes_of(pair):
        return pl.ds(pl.multiple_of(pair * LANES, LANES), LANES)

    def phi(raw, coef):
        value = raw.astype(F32)
        return 0.125 * (value + coef * value * value)

    def compact(full):
        return jnp.where(left, full[:BLOCK], full[BLOCK:])

    def diagonal(value):
        none = jnp.zeros_like(value)
        return jnp.concatenate([jnp.where(left, value, none), jnp.where(left, none, value)], axis=0)

    def weighted(a, weights):
        return (a.astype(F32) * weights).astype(BF16)

    def own_step(pair, carry):
        at = lanes_of(pair)
        coef = coef_ref[:, at]
        q_feat = phi(q_ref[:, at], coef).astype(BF16)
        qf[pl.ds(0, LANES), at] = q_feat
        keys = (phi(k_ref[:, at], coef) * gamma_x[:, at]).astype(BF16)
        wk[:, at] = keys
        logs = lx[pl.ds(0, LANES), at]
        scaled = weighted(g_ref[:, at], jnp.exp(logs))
        gq[:, at] = scaled
        s0 = compact(tn(q_feat[:BLOCK], scaled[:BLOCK]))
        s1 = compact(tn(q_feat[BLOCK:], scaled[BLOCK:]))
        fall0 = jnp.exp(logs[BLOCK - 1 : BLOCK])
        fall1 = jnp.exp(logs[LANES - 1 :])
        s1_out[:, at] = s1.astype(BF16)
        ss_out[:, at] = (s0 + fall0 * s1).astype(BF16)
        values = v_ref[:, at]
        weights = blast_x[pl.ds(0, 3 * BLOCK), at]
        carried0 = weighted(keys[:BLOCK], weights[:BLOCK])
        carried1 = weighted(keys, weights[BLOCK:])
        u0 = compact(tn(carried0, values[:BLOCK]))
        c1 = compact(tn(carried1, values))
        u0c[:, at] = u0
        c1c[:, at] = fall1 * u0 + c1
        s0c[:, at] = s1
        p_out[:, at] = (fall1 * u0 + c1).astype(BF16)
        return carry

    lax.fori_loop(0, PAIRS, own_step, 0)
    send(S_UP)
    send(SS2_UP)
    send(SS3_UP)
    send(P_DN)

    received(L_UP)
    received(Q_UP)
    received(G_UP)
    log_next = lbuf[pl.ds(2 * BLOCK, BLOCK), :]
    log_pair = lbuf[pl.ds(BLOCK, LANES), :]
    block_rows(log_pair, 2, BLOCK)
    lx[pl.ds(LANES, BLOCK), :] = expand(log_next, 3)
    tail2 = jnp.exp(log_next[BLOCK - 1 :] - log_next)
    blast_x[pl.ds(3 * BLOCK, BLOCK), :] = ending(prev_t, tail2)

    def next_step(pair, carry):
        at = lanes_of(pair)
        coef = coef_ref[:, at]
        qf[pl.ds(LANES, BLOCK), at] = phi(qn[:, at], coef).astype(BF16)
        fall2 = jnp.exp(lx[3 * BLOCK - 1 : 3 * BLOCK, at])
        carried = weighted(wk[pl.ds(BLOCK, BLOCK), at], blast_x[pl.ds(3 * BLOCK, BLOCK), at])
        r = compact(tn(carried, v_ref[pl.ds(BLOCK, BLOCK), at]))
        r_out[:, at] = r.astype(BF16)
        t_out[:, at] = (fall2 * c1c[:, at] + r).astype(BF16)
        return carry

    lax.fori_loop(0, PAIRS, next_step, 0)
    send(R_DN)
    send(T2_DN)
    send(T3_DN)

    step = col % BLOCK
    cur_mask = flag(same & (row % BLOCK >= step))
    prev_mask = flag(same & (row % BLOCK < step))
    both_mask = jnp.concatenate([cur_mask, prev_mask], axis=1)
    causal = (iota((3 * BLOCK, LANES), 1) % BLOCK) <= (iota((3 * BLOCK, LANES), 0) % BLOCK)

    def window_step(pair, carry):
        at = lanes_of(pair)
        keys, values = wk[:, at], v_ref[:, at]
        queries = qf[:, at]
        grads = jnp.concatenate([g_ref[:, at], gn[:, at]], axis=0)
        logs = lx[:, at]
        rows = jnp.concatenate(
            [jnp.broadcast_to(lrow[b : b + 1, at], (BLOCK, LANES)) for b in range(3)], axis=0
        )
        decays = jnp.where(causal, jnp.exp(jnp.where(causal, logs - rows, 0.0)), 0.0)
        decays_low = decays.astype(BF16)
        first = nn(decays_low[:BLOCK], cur_mask)
        middle = nn(decays_low[BLOCK:LANES], both_mask)
        final = nn(decays_low[LANES:], prev_mask)
        kernels = (
            jnp.concatenate([first, middle[:, LANES:]], axis=0),
            jnp.concatenate([middle[:, :LANES], final], axis=0),
        )
        d_kernels = []
        d_queries = []
        for block in range(2):
            part = slice(block * BLOCK, (block + 1) * BLOCK)
            span = slice(block * BLOCK, block * BLOCK + LANES)
            keys_bd, values_bd = diagonal(keys[part]), diagonal(values[part])
            scores = nt(queries[span], keys_bd)
            d_weights = nt(grads[span], values_bd).astype(BF16).astype(F32)
            weights = (scores * kernels[block]).astype(BF16)
            d_scores = (d_weights * kernels[block]).astype(BF16)
            d_kernels.append((d_weights * scores).astype(BF16))
            d_queries.append(nn(d_scores, keys_bd))
            dvf[pl.ds(block * BLOCK, BLOCK), at] = compact(tn(weights, grads[span]))
            dwk[pl.ds(block * BLOCK, BLOCK), at] = compact(tn(d_scores, queries[span]))
        dqf[pl.ds(0, BLOCK), at] = d_queries[0][:BLOCK]
        dqf[pl.ds(BLOCK, BLOCK), at] = d_queries[0][BLOCK:] + d_queries[1][:BLOCK]
        dqn_out[:, at] = d_queries[1][BLOCK:].astype(BF16)
        d_decays = jnp.concatenate(
            [
                nt(d_kernels[0][:BLOCK], cur_mask),
                nt(jnp.concatenate([d_kernels[1][:BLOCK], d_kernels[0][BLOCK:]], axis=1), both_mask),
                nt(d_kernels[1][BLOCK:], prev_mask),
            ],
            axis=0,
        )
        gmat[:, at] = (d_decays * decays).astype(BF16)
        return carry

    lax.fori_loop(0, PAIRS, window_step, 0)
    send(DQ_DN)

    for message in (TOT1, TOT2, TOT3, S_UP, SS2_UP, SS3_UP, P_DN, R_DN, T2_DN, T3_DN):
        received(message)
    falls = [expand(tot_in[slot], 3) for slot in range(3)]
    back2 = expand(tot_in[1], 3)
    next1_fall1 = jnp.exp(falls[0][1:2])
    next2_all = jnp.exp(falls[1][0:1] + falls[1][1:2])
    prev1_fall1 = jnp.exp(falls[2][1:2])
    prev1_all = jnp.exp(falls[2][0:1] + falls[2][1:2])
    prev2_fall1 = jnp.exp(back2[1:2])
    own0 = jnp.exp(lx[BLOCK - 1 : BLOCK, :])
    own1 = jnp.exp(lx[LANES - 1 : LANES, :])
    next0 = jnp.exp(lx[3 * BLOCK - 1 :, :])

    memory = (
        p_in[...].astype(F32)
        + prev1_fall1 * t_in[0].astype(F32)
        + (prev2_fall1 * prev1_all) * t_in[1].astype(F32)
    )
    middle_memory = own0 * memory + r_in[...].astype(F32) + u0c[...]
    m_in[...] = memory.astype(BF16)
    m_mid[...] = middle_memory.astype(BF16)
    z = s1_in[...].astype(F32) + next1_fall1 * (
        ss_in[0].astype(F32) + next2_all * ss_in[1].astype(F32)
    )
    z_end[...] = z.astype(BF16)

    def next_adjoint(pair, carry):
        at = lanes_of(pair)
        scaled = weighted(gn[:, at], jnp.exp(lx[pl.ds(LANES, BLOCK), at]))
        c1c[:, at] = compact(tn(qf[pl.ds(LANES, BLOCK), at], scaled))
        return carry

    lax.fori_loop(0, PAIRS, next_adjoint, 0)
    end_grad = next0 * z + c1c[...]
    mid_grad = own1 * end_grad + s0c[...]
    n_end[...] = end_grad.astype(BF16)
    n_mid[...] = mid_grad.astype(BF16)
    fall_grad = jnp.concatenate(
        [
            own0 * jnp.sum(memory * mid_grad, axis=0, keepdims=True),
            own1 * jnp.sum(middle_memory * end_grad, axis=0, keepdims=True),
            jnp.zeros((6, WIDTH), F32),
        ],
        axis=0,
    )
    fall_grad = sum(nt(part, spread) for part in pieces(fall_grad, 2))

    def memory_step(pair, carry):
        at = lanes_of(pair)
        keys, values, scaled = wk[:, at], v_ref[:, at], gq[:, at]
        memory0, memory1 = diagonal(m_in[:, at]), diagonal(m_mid[:, at])
        dq_carried = jnp.concatenate(
            [nt(scaled[:BLOCK], memory0), nt(scaled[BLOCK:], memory1)], axis=0
        )
        dqf[:, at] = dqf[:, at] + dq_carried
        xmat[pl.ds(4 * BLOCK, LANES), at] = (
            dq_carried * qf[pl.ds(0, LANES), at].astype(F32)
        ).astype(BF16)
        grads = [diagonal(ref[:, at]) for ref in (n_mid, n_end, z_end)]
        for block in range(2):
            part = slice(block * BLOCK, (block + 1) * BLOCK)
            both = jnp.concatenate(grads[block : block + 2], axis=0)
            d_carried = nt(values[part], both).astype(BF16).astype(F32)
            own_keys = keys[part].astype(F32)
            d_keys = dwk[pl.ds(block * BLOCK, BLOCK), at]
            carried = []
            for role in range(2):
                index = 2 * block + role
                weights = blast_x[pl.ds(index * BLOCK, BLOCK), at]
                d_role = d_carried[:, role * LANES : (role + 1) * LANES]
                carried.append((own_keys * weights).astype(BF16))
                d_keys = d_keys + d_role * weights
                xmat[pl.ds(index * BLOCK, BLOCK), at] = (d_role * own_keys).astype(BF16)
            dwk[pl.ds(block * BLOCK, BLOCK), at] = d_keys
            dv_ref[pl.ds(block * BLOCK, BLOCK), at] = (
                dvf[pl.ds(block * BLOCK, BLOCK), at] + nn(jnp.concatenate(carried, axis=1), both)
            ).astype(BF16)
        coef = coef_ref[:, at]
        raw = k_ref[:, at].astype(F32)
        d_keys = dwk[:, at]
        d_feat = d_keys * gamma_x[:, at]
        square = 0.125 * raw * raw
        xmat[pl.ds(6 * BLOCK, LANES), at] = (d_keys * (0.125 * raw + coef * square)).astype(BF16)
        dk_ref[:, at] = (d_feat * (0.125 + (0.25 * coef) * raw)).astype(BF16)
        part_ref[32:33, at] = jnp.sum(d_feat * square, axis=0, keepdims=True)
        return carry

    lax.fori_loop(0, PAIRS, memory_step, 0)

    summed = nt(xmat[...], spread)
    lower = flag(scol < srow)
    upper_in = flag(scol >= srow)
    at_or_before = flag(scol <= srow)
    after = flag(scol > srow)

    def twice(mask, a):
        return sum(nn(mask, part) for part in pieces(a, 2))

    def decay_grad(block):
        later = nn(upper_in, gmat[pl.ds(block * BLOCK, BLOCK), :])
        lanes = iota((BLOCK, WIDTH), 1) % BLOCK
        kept = jnp.where(lanes < iota((BLOCK, WIDTH), 0), later, 0.0)
        return sum(nt(part, spread) for part in pieces(kept, 2))

    def tail_grad(block, tail):
        total = 0.0
        if block < 2:
            begin = 0 if block == 0 else 2 * BLOCK
            total = total + twice(at_or_before, summed[begin : begin + BLOCK])
        if block > 0:
            begin = BLOCK if block == 1 else 3 * BLOCK
            total = total + twice(after, summed[begin : begin + BLOCK])
        return twice(lower, total * tail)

    dan_out[...] = decay_grad(2) + tail_grad(2, tail2)
    send(DA_DN)
    d_decay = []
    for block, tail in ((0, tail0), (1, tail1)):
        carried = summed[4 * BLOCK + block * BLOCK : 5 * BLOCK + block * BLOCK]
        d_decay.append(
            decay_grad(block)
            + tail_grad(block, tail)
            + twice(upper_in, carried)
            + fall_grad[block : block + 1]
        )
    received(DA_DN)
    received(DQ_DN)
    d_decay[0] = d_decay[0] + dan_in[...]
    d_decay = jnp.concatenate(d_decay, axis=0)
    gate_row, gate_col = iota((LANES, LANES), 0), iota((LANES, LANES), 1)
    shift = flag(gate_col == gate_row + HEADS)
    d_gamma = sum(nn(part, shift) for part in pieces(summed[6 * BLOCK :], 2))
    is_decay = iota((LANES, LANES), 1) < HEADS
    d_logits = jnp.where(is_decay, -rate * sig * d_decay, d_gamma * gamma * (1.0 - sig))
    rates = jnp.sum(jnp.where(is_decay, -soft * d_decay, 0.0), axis=0, keepdims=True)
    d_hi, d_lo = pieces(d_logits, 2)
    dx_ref[...] = (nn(d_hi, w_hi) + (nn(d_hi, w_lo) + nn(d_lo, w_hi))).astype(BF16)
    gate = tn(d_hi, x) + tn(d_lo, x)
    part_ref[0:32, :] = gate[:32]
    part_ref[33:40, :] = jnp.zeros((7, WIDTH), F32)
    part_ref[33:34, 0:LANES] = rates

    def query_step(pair, carry):
        at = lanes_of(pair)
        coef = coef_ref[:, at]
        raw = q_ref[:, at].astype(F32)
        d_feat = dqf[:, at] + jnp.concatenate(
            [dqn_in[:, at].astype(F32), jnp.zeros((BLOCK, LANES), F32)], axis=0
        )
        dq_ref[:, at] = (d_feat * (0.125 + (0.25 * coef) * raw)).astype(BF16)
        part_ref[32:33, at] = part_ref[32:33, at] + jnp.sum(
            d_feat * (0.125 * raw * raw), axis=0, keepdims=True
        )
        return carry

    lax.fori_loop(0, PAIRS, query_step, 0)
    for message in range(MESSAGES):
        sent(message)


def main_call(queries, keys, values, inputs, gate, coef, rate, cotangent):
    rows = queries.shape[0]
    vmem = pl.BlockSpec(memory_space=pltpu.VMEM)
    block = (BLOCK, WIDTH)
    out = jax.ShapeDtypeStruct((rows, WIDTH), BF16)
    scratch = [
        (block, BF16), (block, BF16), ((3 * BLOCK, LANES), F32), ((8, LANES), F32), ((3, 8, LANES), F32),
        (block, BF16), (block, BF16), (block, BF16), ((2,) + block, BF16),
        (block, BF16), (block, BF16), (block, BF16), (block, BF16), (block, BF16), ((2,) + block, BF16),
        (block, BF16), (block, BF16), ((BLOCK, LANES), F32), ((BLOCK, LANES), F32),
        ((8, WIDTH), F32), ((3 * BLOCK, WIDTH), F32), ((LANES, WIDTH), F32), ((4 * BLOCK, WIDTH), F32),
        ((3 * BLOCK, WIDTH), BF16), ((LANES, WIDTH), BF16), ((LANES, WIDTH), BF16),
        (block, F32), (block, F32), (block, F32),
        (block, BF16), (block, BF16), (block, BF16), (block, BF16), (block, BF16),
        ((LANES, WIDTH), F32), ((LANES, WIDTH), F32), ((LANES, WIDTH), F32),
        ((3 * BLOCK, WIDTH), BF16), ((8 * BLOCK, WIDTH), BF16),
    ]
    return pl.pallas_call(
        main_kernel,
        out_shape=[out, out, out, out, jax.ShapeDtypeStruct((40, WIDTH), F32)],
        in_specs=[vmem] * 8,
        out_specs=[vmem] * 5,
        scratch_shapes=[pltpu.VMEM(shape, dtype) for shape, dtype in scratch]
        + [pltpu.SemaphoreType.DMA((MESSAGES,)), pltpu.SemaphoreType.DMA((MESSAGES,))],
        compiler_params=pltpu.CompilerParams(
            collective_id=0, has_side_effects=True, vmem_limit_bytes=48 * 2**20
        ),
        name="window_backward",
    )(queries, keys, values, inputs, gate, coef, rate, cotangent)


def reduce_kernel(z_size, y_size, part_ref, out_ref, mine, first, second, third, done, acc, send_sem, recv_sem):
    dp, xpos = lax.axis_index("dp"), lax.axis_index("seq")
    z, y, core = dp // (y_size * 2), (dp // 2) % y_size, dp % 2
    eight = xpos * 2 + core

    def octet(hop):
        other = lax.rem(eight + hop, 8)
        return {"dp": (z * y_size + y) * 2 + other % 2, "seq": other // 2}

    def along_y(hop):
        return {"dp": (z * y_size + lax.rem(y + hop, y_size)) * 2 + core, "seq": xpos}

    def along_z(hop):
        return {"dp": (lax.rem(z + hop, z_size) * y_size + y) * 2 + core, "seq": xpos}

    groups = [(octet, 8), (along_y, y_size), (along_z, z_size)]
    barrier = pltpu.get_barrier_semaphore()
    partners = 0
    for where, size in groups:
        for hop in range(1, size):
            pl.semaphore_signal(barrier, inc=1, device_id=where(hop), device_id_type=MESH)
            partners += 1
    for chunk in range(8):
        mine[chunk] = part_ref[:, chunk * LANES : (chunk + 1) * LANES].astype(BF16)
    pl.semaphore_wait(barrier, partners)

    def exchange(base, size, where, source, target):
        made = []
        for hop in range(1, size):
            made.append(
                pltpu.make_async_remote_copy(
                    src_ref=source(hop),
                    dst_ref=target(hop),
                    send_sem=send_sem.at[base + hop],
                    recv_sem=recv_sem.at[base + hop],
                    device_id=where(hop),
                    device_id_type=MESH,
                )
            )
        for made_copy in made:
            made_copy.start()
        return made

    copies = exchange(
        0, 8, octet, lambda hop: mine.at[lax.rem(eight + hop, 8)], lambda hop: first.at[eight]
    )
    first[eight] = mine[eight]
    for made in copies:
        made.wait_recv()
    total = first[0].astype(F32)
    for index in range(1, 8):
        total = total + first[index].astype(F32)
    second[y] = total.astype(BF16)
    more = exchange(8, y_size, along_y, lambda hop: second.at[y], lambda hop: second.at[y])
    for made in more:
        made.wait_recv()
    copies += more
    total = second[0].astype(F32)
    for index in range(1, y_size):
        total = total + second[index].astype(F32)
    third[z] = total.astype(BF16)
    more = exchange(8 + y_size, z_size, along_z, lambda hop: third.at[z], lambda hop: third.at[z])
    for made in more:
        made.wait_recv()
    copies += more
    total = third[0].astype(F32)
    for index in range(1, z_size):
        total = total + third[index].astype(F32)
    done[eight] = total.astype(BF16)
    more = exchange(
        8 + y_size + z_size, 8, octet, lambda hop: done.at[eight], lambda hop: done.at[eight]
    )
    for made in more:
        made.wait_recv()
    copies += more
    for chunk in range(8):
        out_ref[:, chunk * LANES : (chunk + 1) * LANES] = done[chunk].astype(F32)
    for made in copies:
        made.wait_send()


def reduce_call(part, z_size, y_size):
    vmem = pl.BlockSpec(memory_space=pltpu.VMEM)
    chunk = (part.shape[0], LANES)
    count = 16 + y_size + z_size
    return pl.pallas_call(
        functools.partial(reduce_kernel, z_size, y_size),
        out_shape=jax.ShapeDtypeStruct(part.shape, F32),
        in_specs=[vmem],
        out_specs=vmem,
        scratch_shapes=[
            pltpu.VMEM((8,) + chunk, BF16),
            pltpu.VMEM((8,) + chunk, BF16),
            pltpu.VMEM((y_size,) + chunk, BF16),
            pltpu.VMEM((z_size,) + chunk, BF16),
            pltpu.VMEM((8,) + chunk, BF16),
            pltpu.VMEM(chunk, F32),
            pltpu.SemaphoreType.DMA((count,)),
            pltpu.SemaphoreType.DMA((count,)),
        ],
        compiler_params=pltpu.CompilerParams(
            collective_id=1, has_side_effects=True, vmem_limit_bytes=16 * 2**20
        ),
        name="sum_parameters",
    )(part)


def on_device(z_size, y_size, queries, keys, values, inputs, gate, coef, rate, cotangent):
    dq, dk, dv, dx, part = main_call(
        queries[0], keys[0], values[0], inputs[0], gate.T, coef[None], rate[None], cotangent[0]
    )
    if z_size:
        total = reduce_call(part, z_size, y_size)
    else:
        total = lax.psum(part, ("dp", "seq"))
    return (
        dq[None], dk[None], dv[None], dx[None],
        total[:32].T, total[32], total[33, :HEADS],
    )


def solution(mesh):
    rows = P("dp", "seq", None)
    sizes = (8, 4) if mesh.shape["dp"] == 64 else (0, 0)
    return jax.shard_map(
        functools.partial(on_device, *sizes),
        mesh=mesh,
        in_specs=(rows, rows, rows, rows, P(), P(), P(), rows),
        out_specs=(rows, rows, rows, rows, P(), P(), P()),
        check_vma=False,
    )
```

time: 440 us -> 66 us (0.15)
  waiting for transfers between devices: 148 us -> 0 us
  blocking collectives: 121 us -> 0 us
  local copies, waits for them, and re-layouts: 73.8 us -> 10.9 us
  Pallas kernels: 0 us -> 54.1 us
  matrix products: 35.3 us -> 0 us
  other arithmetic: 27.4 us -> 0 us
  between operations: 15.4 us -> 0.68 us
  starting transfers between devices: 14.7 us -> 0 us
    psum x1 -> x0, waiting for transfers between devices: 148 us -> none  [on_device(): totals = lax.psum((grads[4], grads[5], grads[6]), ('dp', 'seq'))]
    psum x1 -> x0, blocking collectives: 90.7 us -> none  [on_device(): totals = lax.psum((grads[4], grads[5], grads[6]), ('dp', 'seq'))]
    pallas_call x0 -> x2, Pallas kernels: none -> 54.1 us  [the longest x1 29.3 us: reduce_call(): pl.pallas_call(functools.partial(reduce_kernel, z_size, y_size), out_shap...]
    dot_general x35 -> x0, matrix products: 35.3 us -> none  [the longest x8 15 us: block_step(): jnp.einsum('thd,hde->the', q_heads.astype(jnp.float32), memory, precision...]
    all_gather x2 -> x0, blocking collectives: 23.3 us -> none  [the longest x1 12 us: entering(): lax.all_gather(part.astype(kind), axis)]
    while x116 -> x0, local copies, waits for them, and re-layouts: 20.7 us -> none
    ppermute x6 -> x0, starting transfers between devices: 14.7 us -> none  [passed_along(): lax.ppermute(value, axis, [(source, source + steps) for source in range(f...]
    dynamic_slice x24 -> x0, local copies, waits for them, and re-layouts: 12.9 us -> none  [the longest x18 8.46 us: local_forward(): lax.scan(block_step, memory, (query_feat.reshape(blocks, window, width_al...]
  transfers between devices with their start and end apart: 7 -> 0, of which waited for: 1 -> 0; matrix products, arithmetic and copies ran while one was open for 3% -> 0% of each run, Pallas kernels for 0% -> 0%
where the time goes in v1:
time: 66 us; the launch traced here: 65.7 us
  Pallas kernels  54.1 us (82%)
  local copies, waits for them, and re-layouts  10.9 us (17%)
  between operations  0.68 us (1%)
    pallas_call x1, Pallas kernels, reduce_call(): pl.pallas_call(functools.partial(reduce_kernel, z_size, y_size), out_shap...  29.3 us
    pallas_call x1, Pallas kernels, main_call(): pl.pallas_call(main_kernel, out_shape=[out, out, out, out, jax.ShapeDtype...  24.8 us
    unnamed x20, local copies, waits for them, and re-layouts  9.13 us

profile of v1, /device:TPU:1, one launch (start us, length us, event | category | flops | bytes accessed | tf_op | source)
XLA Modules:
  0.0 65.7 jit_solution(13958677012053498531)
XLA Ops:
  0.6 0.0 copy-start.6
  0.6 0.0 copy-start.7
  0.7 0.7 %copy-done.6 = f32[1024]{0:T(1024)S(1)} copy-done((f32[1024]{0:T(1024)S(1)}, f32[1024]{0:T(1024)}, u32[]{:S(2)}) %copy-start.6) | copy-done | bytes 4120
  1.3 0.0 copy-done.7
  1.3 0.0 copy-start
  1.3 0.9 %copy-done = bf16[1,128,1024]{2,1,0:T(8,128)(2,1)S(1)} copy-done((bf16[1,128,1024]{2,1,0:T(8,128)(2,1)S(1)}, bf16[1,128,1024]{2,1,0:T(8,128)(2,1)}, u32[]{:S(2)}) %copy-start) | copy-done | bytes 262168
  2.3 0.0 copy-start.1
  2.3 0.9 %copy-done.1 = bf16[1,128,1024]{2,1,0:T(8,128)(2,1)S(1)} copy-done((bf16[1,128,1024]{2,1,0:T(8,128)(2,1)S(1)}, bf16[1,128,1024]{2,1,0:T(8,128)(2,1)}, u32[]{:S(2)}) %copy-start.1) | copy-done | bytes 262168
  3.2 0.0 copy-start.2
  3.2 0.9 %copy-done.2 = bf16[1,128,1024]{2,1,0:T(8,128)(2,1)S(1)} copy-done((bf16[1,128,1024]{2,1,0:T(8,128)(2,1)S(1)}, bf16[1,128,1024]{2,1,0:T(8,128)(2,1)}, u32[]{:S(2)}) %copy-start.2) | copy-done | bytes 262168
  4.2 0.0 copy-start.3
  4.2 0.9 %copy-done.3 = bf16[1,128,1024]{2,1,0:T(8,128)(2,1)S(1)} copy-done((bf16[1,128,1024]{2,1,0:T(8,128)(2,1)S(1)}, bf16[1,128,1024]{2,1,0:T(8,128)(2,1)}, u32[]{:S(2)}) %copy-start.3) | copy-done | bytes 262168
  5.1 0.0 copy-start.4
  5.1 0.9 %copy-done.4 = bf16[1,128,1024]{2,1,0:T(8,128)(2,1)S(1)} copy-done((bf16[1,128,1024]{2,1,0:T(8,128)(2,1)S(1)}, bf16[1,128,1024]{2,1,0:T(8,128)(2,1)}, u32[]{:S(2)}) %copy-start.4) | copy-done | bytes 262168
  6.1 0.0 copy-start.5
  6.1 0.9 %copy-done.5 = f32[1024,32]{0,1:T(8,128)S(1)} copy-done((f32[1024,32]{0,1:T(8,128)S(1)}, f32[1024,32]{0,1:T(8,128)}, u32[]{:S(2)}) %copy-start.5) | copy-done | bytes 131096
  7.0 24.8 %window_backward.1 = (bf16[128,1024]{1,0:T(8,128)(2,1)S(1)}, bf16[128,1024]{1,0:T(8,128)(2,1)S(1)}, bf16[128,1024]{1,0:T(8,128)(2,1)S(1)}, bf16[128,1024]{1,0:T(8,128)(2,1)S(1)}, f32[40,1024]{1,0:T(8,128)S(1)}) custom-call(bf16[128,1024]{1,0:T(8,128)(2,1)S(1)} %bitcast.21, bf16[128,1024]{1,0:T(8,128)(2,1)S(1)} %bitcast.22, bf16[128,1024]{1,0:T(8,128)(2,1)S(1)} %bitcast.23, ...), custom_call_target="tpu_custom_call" | custom-call | tf_op jit(solution)/shard_map/window_backward/pallas_call | solution.py:517
  31.8 29.3 %sum_parameters.1 = f32[40,1024]{1,0:T(8,128)S(1)} custom-call(f32[40,1024]{1,0:T(8,128)S(1)} %get-tuple-element.16.part_ref), custom_call_target="tpu_custom_call" | custom-call | tf_op jit(solution)/shard_map/sum_parameters/pallas_call | solution.py:616
  61.1 0.7 %slice_bitcast_fusion = f32[1024,32]{0,1:T(8,128)} fusion(f32[40,1024]{1,0:T(8,128)S(1)} %sum_parameters.1), kind=kLoop, calls=%fused_computation | loop fusion | bytes 262144 | tf_op jit(solution)/shard_map/transpose | solution.py:648
  61.8 0.6 slice.10
  62.4 0.5 slice_bitcast_fusion.1
  62.9 0.7 %copy.19 = bf16[1,128,1024]{2,1,0:T(8,128)(2,1)} copy(bf16[1,128,1024]{2,1,0:T(8,128)(2,1)S(1)} %bitcast.20) | data formatting | bytes 524288
  63.6 0.7 %copy.20 = bf16[1,128,1024]{2,1,0:T(8,128)(2,1)} copy(bf16[1,128,1024]{2,1,0:T(8,128)(2,1)S(1)} %bitcast.19) | data formatting | bytes 524288
  64.3 0.7 %copy.21 = bf16[1,128,1024]{2,1,0:T(8,128)(2,1)} copy(bf16[1,128,1024]{2,1,0:T(8,128)(2,1)S(1)} %bitcast.18) | data formatting | bytes 524288
  65.0 0.7 %copy.22 = bf16[1,128,1024]{2,1,0:T(8,128)(2,1)} copy(bf16[1,128,1024]{2,1,0:T(8,128)(2,1)S(1)} %bitcast.17) | data formatting | bytes 524288
Async XLA Ops:
  0.6 0.7 %copy-start.6 = (f32[1024]{0:T(1024)S(1)}, f32[1024]{0:T(1024)}, u32[]{:S(2)}) copy-start(f32[1024]{0:T(1024)} %param.13) | copy-start | bytes 12292
  0.6 0.7 %copy-start.7 = (f32[16]{0:T(128)S(1)}, f32[16]{0:T(128)}, u32[]{:S(2)}) copy-start(f32[16]{0:T(128)} %param.14) | copy-start | bytes 196
  1.3 1.0 %copy-start = (bf16[1,128,1024]{2,1,0:T(8,128)(2,1)S(1)}, bf16[1,128,1024]{2,1,0:T(8,128)(2,1)}, u32[]{:S(2)}) copy-start(bf16[1,128,1024]{2,1,0:T(8,128)(2,1)} %param.8) | copy-start | bytes 786436
  2.3 0.9 %copy-start.1 = (bf16[1,128,1024]{2,1,0:T(8,128)(2,1)S(1)}, bf16[1,128,1024]{2,1,0:T(8,128)(2,1)}, u32[]{:S(2)}) copy-start(bf16[1,128,1024]{2,1,0:T(8,128)(2,1)} %param.9) | copy-start | bytes 786436
  3.2 0.9 %copy-start.2 = (bf16[1,128,1024]{2,1,0:T(8,128)(2,1)S(1)}, bf16[1,128,1024]{2,1,0:T(8,128)(2,1)}, u32[]{:S(2)}) copy-start(bf16[1,128,1024]{2,1,0:T(8,128)(2,1)} %param.10) | copy-start | bytes 786436
  4.2 0.9 %copy-start.3 = (bf16[1,128,1024]{2,1,0:T(8,128)(2,1)S(1)}, bf16[1,128,1024]{2,1,0:T(8,128)(2,1)}, u32[]{:S(2)}) copy-start(bf16[1,128,1024]{2,1,0:T(8,128)(2,1)} %param.11) | copy-start | bytes 786436
  5.1 0.9 %copy-start.4 = (bf16[1,128,1024]{2,1,0:T(8,128)(2,1)S(1)}, bf16[1,128,1024]{2,1,0:T(8,128)(2,1)}, u32[]{:S(2)}) copy-start(bf16[1,128,1024]{2,1,0:T(8,128)(2,1)} %param.15) | copy-start | bytes 786436
  6.1 0.9 %copy-start.5 = (f32[1024,32]{0,1:T(8,128)S(1)}, f32[1024,32]{0,1:T(8,128)}, u32[]{:S(2)}) copy-start(f32[1024,32]{0,1:T(8,128)} %param.12) | copy-start | bytes 393220

commit v2 on v1

v2 whole, which is shorter than its diff:
```python
import functools

import jax
import jax.numpy as jnp
from jax import lax
from jax.experimental import pallas as pl
from jax.experimental.pallas import tpu as pltpu
from jax.sharding import PartitionSpec as P

BLOCK = 64
LANES = 128
WIDTH = 1024
PAIRS = WIDTH // LANES
HEADS = 16
F32 = jnp.float32
BF16 = jnp.bfloat16
MESH = pl.DeviceIdType.MESH


def nn(a, b):
    return lax.dot_general(a, b, (((1,), (0,)), ((), ())), preferred_element_type=F32)


def nt(a, b):
    return lax.dot_general(a, b, (((1,), (1,)), ((), ())), preferred_element_type=F32)


def tn(a, b):
    return lax.dot_general(a, b, (((0,), (0,)), ((), ())), preferred_element_type=F32)


def pieces(a, count):
    parts = []
    for _ in range(count):
        part = a.astype(BF16)
        parts.append(part)
        a = a - part.astype(F32)
    return parts


def flag(condition):
    return jnp.where(condition, 1.0, 0.0).astype(BF16)


def iota(shape, dimension):
    return lax.broadcasted_iota(jnp.int32, shape, dimension)


Q_UP, G_UP, L_UP, S_UP, SS2_UP, SS3_UP, TOT1, TOT2, TOT3 = range(9)
P_DN, R_DN, T2_DN, T3_DN, DQ_DN, DA_DN = range(9, 15)
MESSAGES = 15
LOADS = 8
TALL = 48


def main_kernel(
    z_size, y_size,
    q_hbm, k_hbm, v_hbm, x_hbm, w_hbm, coef_hbm, rate_hbm, g_hbm,
    dq_ref, dk_ref, dv_ref, dx_ref, gate_ref, coef_out, rate_out,
    q_ref, k_ref, v_ref, x_ref, g_ref, w_ref, coef_ref, rate_ref,
    qn, gn, lbuf, tot, tot_in, s1_out, ss_out, s1_in, ss_in, p_out, r_out, t_out, p_in, r_in, t_in,
    dqn_out, dqn_in, dan_out, dan_in,
    lrow, lx, gamma_x, blast_x, qf, wk, gq, s1c, u0c, c1c, m_in, m_mid, n_mid, n_end, z_end,
    dqf, dwk, dvf, gmat, xmat, coef_sum,
    mine, first, second, third, done,
    load_sem, send_sem, recv_sem, sum_send, sum_recv,
):
    place, dp = lax.axis_index("seq"), lax.axis_index("dp")
    z, y, core = dp // (y_size * 2), (dp // 2) % y_size, dp % 2
    last = 3

    loads = [
        pltpu.make_async_copy(source, target, load_sem.at[index])
        for index, (source, target) in enumerate(
            (
                (x_hbm, x_ref), (w_hbm, w_ref), (rate_hbm, rate_ref), (coef_hbm, coef_ref),
                (k_hbm, k_ref), (q_hbm, q_ref), (v_hbm, v_ref), (g_hbm, g_ref),
            )
        )
    ]
    for load in loads:
        load.start()
    def copy(source, target, message, to):
        return pltpu.make_async_remote_copy(
            src_ref=source,
            dst_ref=target,
            send_sem=send_sem.at[message],
            recv_sem=recv_sem.at[message],
            device_id={"seq": to},
            device_id_type=MESH,
        )

    up1, up2, up3 = place - 1, place - 2, place - 3
    dn1, dn2, dn3 = place + 1, place + 2, place + 3
    around = [lax.rem(place + 4 - hop, 4) for hop in (1, 2, 3)]
    copies = {
        Q_UP: (copy(q_ref.at[pl.ds(0, BLOCK)], qn, Q_UP, up1), 1),
        G_UP: (copy(g_ref.at[pl.ds(0, BLOCK)], gn, G_UP, up1), 1),
        L_UP: (copy(lbuf.at[pl.ds(0, BLOCK)], lbuf.at[pl.ds(2 * BLOCK, BLOCK)], L_UP, up1), 1),
        S_UP: (copy(s1_out, s1_in, S_UP, up1), 1),
        SS2_UP: (copy(ss_out, ss_in.at[0], SS2_UP, up2), 2),
        SS3_UP: (copy(ss_out, ss_in.at[1], SS3_UP, up3), 3),
        TOT1: (copy(tot, tot_in.at[0], TOT1, around[0]), 0),
        TOT2: (copy(tot, tot_in.at[1], TOT2, around[1]), 0),
        TOT3: (copy(tot, tot_in.at[2], TOT3, around[2]), 0),
        P_DN: (copy(p_out, p_in, P_DN, dn1), -1),
        R_DN: (copy(r_out, r_in, R_DN, dn1), -1),
        T2_DN: (copy(t_out, t_in.at[0], T2_DN, dn2), -2),
        T3_DN: (copy(t_out, t_in.at[1], T3_DN, dn3), -3),
        DQ_DN: (copy(dqn_out, dqn_in, DQ_DN, dn1), -1),
        DA_DN: (copy(dan_out, dan_in, DA_DN, dn1), -1),
    }

    def guarded(steps, action):
        if steps == 0:
            action()
        elif steps > 0:
            pl.when(place >= steps)(action)
        else:
            pl.when(place <= last + steps)(action)

    def send(*messages):
        for message in messages:
            description, steps = copies[message]
            guarded(steps, description.start)

    def sent(message):
        description, steps = copies[message]
        guarded(steps, description.wait_send)

    def received(*messages):
        for message in messages:
            description, steps = copies[message]
            guarded(-steps, description.wait_recv)

    eight = place * 2 + core

    def octet(hop):
        other = lax.rem(eight + hop, 8)
        return {"dp": (z * y_size + y) * 2 + other % 2, "seq": other // 2}

    def along_y(hop):
        return {"dp": (z * y_size + lax.rem(y + hop, y_size)) * 2 + core, "seq": place}

    def along_z(hop):
        return {"dp": (lax.rem(z + hop, z_size) * y_size + y) * 2 + core, "seq": place}

    barrier = pltpu.get_barrier_semaphore()
    partners = 0
    for where, size in ((octet, 8), (along_y, y_size), (along_z, z_size)):
        for hop in range(1, size):
            pl.semaphore_signal(barrier, inc=1, device_id=where(hop), device_id_type=MESH)
            partners += 1

    @pl.when(place == last)
    def _():
        qn[...] = jnp.zeros_like(qn)
        gn[...] = jnp.zeros_like(gn)
        lbuf[pl.ds(2 * BLOCK, BLOCK), :] = jnp.zeros((BLOCK, LANES), F32)
        s1_in[...] = jnp.zeros_like(s1_in)

    for hop in (2, 3):
        @pl.when(place > last - hop)
        def _():
            ss_in[hop - 2] = jnp.zeros(ss_in.shape[1:], BF16)

        @pl.when(place < hop)
        def _():
            t_in[hop - 2] = jnp.zeros(t_in.shape[1:], BF16)

    @pl.when(place == 0)
    def _():
        p_in[...] = jnp.zeros_like(p_in)
        r_in[...] = jnp.zeros_like(r_in)
        dqn_in[...] = jnp.zeros_like(dqn_in)
        dan_in[...] = jnp.zeros_like(dan_in)

    row, col = iota((LANES, LANES), 0), iota((LANES, LANES), 1)
    same = (row // BLOCK) == (col // BLOCK)
    tri = flag(same & (col <= row))
    head_row = iota((LANES, WIDTH), 0)
    head_lane = iota((LANES, WIDTH), 1) // BLOCK
    spread = flag(head_row == head_lane)
    spread_gate = flag(head_row == head_lane + HEADS)
    left = iota((BLOCK, LANES), 1) < BLOCK
    left1 = iota((1, LANES), 1) < BLOCK
    srow, scol = iota((BLOCK, BLOCK), 0), iota((BLOCK, BLOCK), 1)
    upper_in = flag(scol >= srow)
    lower = flag(scol < srow)
    at_or_before = flag(scol <= srow)
    after = flag(scol > srow)

    loads[0].wait()
    loads[1].wait()
    loads[2].wait()
    w_hi, w_lo = pieces(
        jnp.concatenate([w_ref[...], jnp.zeros((LANES - 2 * HEADS, WIDTH), F32)], axis=0), 2
    )
    x = x_ref[...]
    logits = nt(x, w_hi) + nt(x, w_lo)
    small = jnp.exp(-jnp.abs(logits))
    soft = jnp.maximum(logits, 0.0) + jnp.log1p(small)
    sig = jnp.where(logits >= 0.0, 1.0, small) / (1.0 + small)
    rate = jnp.concatenate([rate_ref[...], jnp.zeros((1, LANES - HEADS), F32)], axis=1)
    decay = -rate * soft
    gamma = sig * (1.0 / BLOCK)
    log_own = sum(nn(tri, part) for part in pieces(decay, 3))
    lbuf[pl.ds(0, LANES), :] = log_own
    tot[...] = jnp.zeros_like(tot)
    tot[0:1, :] = log_own[BLOCK - 1 : BLOCK]
    tot[1:2, :] = log_own[LANES - 1 :]

    def expand(a, count):
        return sum(nn(part, spread) for part in pieces(a, count))

    def block_rows(logs, block, offset):
        pick = flag(row == (col % BLOCK) + offset)
        turned = sum(tn(part, pick) for part in pieces(logs, 3))
        for pair in range(PAIRS):
            lrow[block : block + 1, pl.ds(pair * LANES, LANES)] = jnp.where(
                left1, turned[2 * pair : 2 * pair + 1], turned[2 * pair + 1 : 2 * pair + 2]
            )

    lx[pl.ds(0, LANES), :] = expand(log_own, 3)
    gamma_x[...] = sum(nn(part, spread_gate) for part in pieces(gamma, 2))

    tail0 = jnp.exp(log_own[BLOCK - 1 : BLOCK] - log_own[:BLOCK])
    tail1 = jnp.exp(log_own[LANES - 1 :] - log_own[BLOCK:])

    def ending(mask, tail):
        return expand(sum(nn(mask, part) for part in pieces(tail, 2)), 2)

    blast_x[pl.ds(0, BLOCK), :] = ending(upper_in, tail0)
    blast_x[pl.ds(BLOCK, BLOCK), :] = ending(lower, tail1)
    blast_x[pl.ds(2 * BLOCK, BLOCK), :] = ending(upper_in, tail1)

    def each_pair(step):
        lax.fori_loop(0, PAIRS, step, 0, unroll=PAIRS)

    def lanes_of(pair):
        return pl.ds(pl.multiple_of(pair * LANES, LANES), LANES)

    def phi(raw, coef):
        value = raw.astype(F32)
        return 0.125 * (value + coef * value * value)

    def compact(full):
        return jnp.where(left, full[:BLOCK], full[BLOCK:])

    def diagonal(value):
        none = jnp.zeros_like(value)
        return jnp.concatenate([jnp.where(left, value, none), jnp.where(left, none, value)], axis=0)

    def weighted(a, weights):
        return (a.astype(F32) * weights).astype(BF16)

    for load in loads[3:]:
        load.wait()

    def own_step(pair, carry):
        at = lanes_of(pair)
        coef = coef_ref[:, at]
        q_feat = phi(q_ref[:, at], coef).astype(BF16)
        qf[pl.ds(0, LANES), at] = q_feat
        keys = (phi(k_ref[:, at], coef) * gamma_x[:, at]).astype(BF16)
        wk[:, at] = keys
        logs = lx[pl.ds(0, LANES), at]
        scaled = weighted(g_ref[:, at], jnp.exp(logs))
        gq[:, at] = scaled
        s0 = compact(tn(q_feat[:BLOCK], scaled[:BLOCK]))
        s1 = compact(tn(q_feat[BLOCK:], scaled[BLOCK:]))
        fall0 = jnp.exp(logs[BLOCK - 1 : BLOCK])
        fall1 = jnp.exp(logs[LANES - 1 :])
        s1_out[:, at] = s1.astype(BF16)
        ss_out[:, at] = (s0 + fall0 * s1).astype(BF16)
        values = v_ref[:, at]
        weights = blast_x[pl.ds(0, 3 * BLOCK), at]
        carried0 = weighted(keys[:BLOCK], weights[:BLOCK])
        carried1 = weighted(keys, weights[BLOCK:])
        u0 = compact(tn(carried0, values[:BLOCK]))
        c1 = fall1 * u0 + compact(tn(carried1, values))
        u0c[:, at] = u0
        c1c[:, at] = c1
        s1c[:, at] = s1
        p_out[:, at] = c1.astype(BF16)
        return carry

    each_pair(own_step)
    pl.semaphore_wait(barrier, partners)
    send(L_UP, TOT1, TOT2, TOT3, Q_UP, G_UP, S_UP, SS2_UP, SS3_UP, P_DN)

    block_rows(log_own, 0, 0)
    block_rows(log_own, 1, BLOCK)

    step = col % BLOCK
    cur_mask = flag(same & (row % BLOCK >= step))
    prev_mask = flag(same & (row % BLOCK < step))
    both_mask = jnp.concatenate([cur_mask, prev_mask], axis=1)
    causal = (iota((LANES, LANES), 1) % BLOCK) <= (iota((LANES, LANES), 0) % BLOCK)

    def spans(rows):
        return pl.ds(rows.start, rows.stop - rows.start)

    first_rows, last_rows = slice(0, BLOCK), slice(BLOCK, LANES)

    def tile(keys_bd, values_bd, queries, grads, kernel):
        scores = nt(queries, keys_bd)
        d_weights = nt(grads, values_bd).astype(BF16).astype(F32)
        weights = (scores * kernel).astype(BF16)
        d_scores = (d_weights * kernel).astype(BF16)
        d_kernel = (d_weights * scores).astype(BF16)
        return (
            nn(d_scores, keys_bd),
            compact(tn(weights, grads)),
            compact(tn(d_scores, queries)),
            d_kernel,
        )

    def window_step(pair, carry):
        at = lanes_of(pair)
        keys, values = wk[:, at], v_ref[:, at]
        queries, grads = qf[pl.ds(0, LANES), at], g_ref[:, at]
        rows = jnp.concatenate(
            [jnp.broadcast_to(lrow[b : b + 1, at], (BLOCK, LANES)) for b in range(2)], axis=0
        )
        gaps = jnp.where(causal, lx[pl.ds(0, LANES), at] - rows, 0.0)
        decays = jnp.where(causal, jnp.exp(gaps), 0.0)
        low = decays.astype(BF16)
        start = nn(low[:BLOCK], cur_mask)
        middle = nn(low[BLOCK:], both_mask)
        dq0, dv0, dk0, db0 = tile(
            diagonal(keys[:BLOCK]), diagonal(values[:BLOCK]), queries, grads,
            jnp.concatenate([start, middle[:, LANES:]], axis=0),
        )
        dq1, dv1, dk1, db1 = tile(
            diagonal(keys[BLOCK:]), diagonal(values[BLOCK:]), queries[BLOCK:], grads[BLOCK:],
            middle[:, :LANES],
        )
        dvf[pl.ds(0, BLOCK), at] = dv0
        dvf[pl.ds(BLOCK, BLOCK), at] = dv1
        dwk[pl.ds(0, BLOCK), at] = dk0
        dwk[pl.ds(BLOCK, BLOCK), at] = dk1
        dqf[pl.ds(0, BLOCK), at] = dq0[:BLOCK]
        dqf[pl.ds(BLOCK, BLOCK), at] = dq0[BLOCK:] + dq1
        d_decays = jnp.concatenate(
            [
                nt(db0[:BLOCK], cur_mask),
                nt(jnp.concatenate([db1, db0[BLOCK:]], axis=1), both_mask),
            ],
            axis=0,
        )
        gmat[pl.ds(0, LANES), at] = (d_decays * decays).astype(BF16)
        return carry

    received(L_UP)
    log_next = lbuf[pl.ds(2 * BLOCK, BLOCK), :]
    lx[pl.ds(LANES, BLOCK), :] = expand(log_next, 3)
    tail2 = jnp.exp(log_next[BLOCK - 1 :] - log_next)
    blast_x[pl.ds(3 * BLOCK, BLOCK), :] = ending(lower, tail2)

    def next_step(pair, carry):
        at = lanes_of(pair)
        fall2 = jnp.exp(lx[3 * BLOCK - 1 : 3 * BLOCK, at])
        carried = weighted(wk[pl.ds(BLOCK, BLOCK), at], blast_x[pl.ds(3 * BLOCK, BLOCK), at])
        r = compact(tn(carried, v_ref[pl.ds(BLOCK, BLOCK), at]))
        r_out[:, at] = r.astype(BF16)
        t_out[:, at] = (fall2 * c1c[:, at] + r).astype(BF16)
        return carry

    each_pair(next_step)
    send(T2_DN, T3_DN, R_DN)

    each_pair(window_step)
    block_rows(lbuf[pl.ds(BLOCK, LANES), :], 2, BLOCK)

    received(Q_UP, G_UP)

    def cross_step(pair, carry):
        at = lanes_of(pair)
        queries = phi(qn[:, at], coef_ref[:, at]).astype(BF16)
        grads = gn[:, at]
        logs = lx[pl.ds(LANES, BLOCK), at]
        held = causal[:BLOCK]
        decays = jnp.where(held, jnp.exp(jnp.where(held, logs - lrow[2:3, at], 0.0)), 0.0)
        dq, dv, dk, db = tile(
            diagonal(wk[pl.ds(BLOCK, BLOCK), at]), diagonal(v_ref[pl.ds(BLOCK, BLOCK), at]),
            queries, grads, nn(decays.astype(BF16), prev_mask),
        )
        dqn_out[:, at] = dq.astype(BF16)
        dvf[pl.ds(BLOCK, BLOCK), at] = dvf[pl.ds(BLOCK, BLOCK), at] + dv
        dwk[pl.ds(BLOCK, BLOCK), at] = dwk[pl.ds(BLOCK, BLOCK), at] + dk
        gmat[pl.ds(LANES, BLOCK), at] = (nt(db, prev_mask) * decays).astype(BF16)
        c1c[:, at] = compact(tn(queries, weighted(grads, jnp.exp(logs))))
        return carry

    each_pair(cross_step)
    send(DQ_DN)

    def decay_grad(block):
        later = nn(upper_in, gmat[pl.ds(block * BLOCK, BLOCK), :])
        lanes = iota((BLOCK, WIDTH), 1) % BLOCK
        kept = jnp.where(lanes < iota((BLOCK, WIDTH), 0), later, 0.0)
        return sum(nt(part, spread) for part in pieces(kept, 2))

    def twice(mask, a):
        return sum(nn(mask, part) for part in pieces(a, 2))

    received(TOT1, S_UP, TOT2, SS2_UP, SS3_UP, TOT3)
    falls = [expand(tot_in[slot], 3) for slot in range(3)]
    next1_fall1 = jnp.exp(falls[0][1:2])
    next2_all = jnp.exp(falls[1][0:1] + falls[1][1:2])
    prev1_fall1 = jnp.exp(falls[2][1:2])
    prev1_all = jnp.exp(falls[2][0:1] + falls[2][1:2])
    prev2_fall1 = jnp.exp(falls[1][1:2])
    own0 = jnp.exp(lx[BLOCK - 1 : BLOCK, :])
    own1 = jnp.exp(lx[LANES - 1 : LANES, :])
    next0 = jnp.exp(lx[3 * BLOCK - 1 :, :])
    z_grad = s1_in[...].astype(F32) + next1_fall1 * (
        ss_in[0].astype(F32) + next2_all * ss_in[1].astype(F32)
    )
    z_end[...] = z_grad.astype(BF16)
    end_grad = next0 * z_grad + c1c[...]
    mid_grad = own1 * end_grad + s1c[...]
    n_end[...] = end_grad.astype(BF16)
    n_mid[...] = mid_grad.astype(BF16)

    def enter(index, keys, d_role, at):
        weights = blast_x[pl.ds(index * BLOCK, BLOCK), at]
        own_keys = keys.astype(F32)
        d_role = d_role.astype(BF16).astype(F32)
        xmat[pl.ds(index * BLOCK, BLOCK), at] = (d_role * own_keys).astype(BF16)
        return (own_keys * weights).astype(BF16), d_role * weights

    def outer_step(pair, carry):
        at = lanes_of(pair)
        rows = pl.ds(BLOCK, BLOCK)
        grads = diagonal(z_end[:, at])
        carried, d_keys = enter(3, wk[rows, at], nt(v_ref[rows, at], grads), at)
        dwk[rows, at] = dwk[rows, at] + d_keys
        dvf[rows, at] = dvf[rows, at] + nn(carried, grads)
        return carry

    each_pair(outer_step)
    d_last = nt(xmat[pl.ds(3 * BLOCK, BLOCK), :], spread)
    dan_out[...] = decay_grad(2) + twice(lower, twice(after, d_last) * tail2)
    send(DA_DN)

    def inner_step(pair, carry):
        at = lanes_of(pair)
        keys, values = wk[:, at], v_ref[:, at]
        grads_end = diagonal(n_end[:, at])
        both = jnp.concatenate([diagonal(n_mid[:, at]), grads_end], axis=0)
        d_first = nt(values[:BLOCK], both)
        carried0, d_keys0 = enter(0, keys[:BLOCK], d_first[:, :LANES], at)
        carried1, d_keys1 = enter(1, keys[:BLOCK], d_first[:, LANES:], at)
        carried2, d_keys2 = enter(2, keys[BLOCK:], nt(values[BLOCK:], grads_end), at)
        dv_ref[pl.ds(0, BLOCK), at] = (
            dvf[pl.ds(0, BLOCK), at] + nn(jnp.concatenate([carried0, carried1], axis=1), both)
        ).astype(BF16)
        dv_ref[pl.ds(BLOCK, BLOCK), at] = (
            dvf[pl.ds(BLOCK, BLOCK), at] + nn(carried2, grads_end)
        ).astype(BF16)
        d_keys = dwk[:, at] + jnp.concatenate([d_keys0 + d_keys1, d_keys2], axis=0)
        coef = coef_ref[:, at]
        raw = k_ref[:, at].astype(F32)
        d_feat = d_keys * gamma_x[:, at]
        square = 0.125 * raw * raw
        xmat[pl.ds(6 * BLOCK, LANES), at] = (d_keys * (0.125 * raw + coef * square)).astype(BF16)
        dk_ref[:, at] = (d_feat * (0.125 + (0.25 * coef) * raw)).astype(BF16)
        coef_sum[0:1, at] = jnp.sum(d_feat * square, axis=0, keepdims=True)
        return carry

    each_pair(inner_step)
    d_enter = nt(xmat[pl.ds(0, 3 * BLOCK), :], spread)
    d_gate = nt(xmat[pl.ds(6 * BLOCK, LANES), :], spread)
    shift = flag(col == row + HEADS)
    d_gamma = sum(nn(part, shift) for part in pieces(d_gate, 2))
    d_decay0 = decay_grad(0) + twice(lower, twice(at_or_before, d_enter[:BLOCK]) * tail0)
    d_decay1 = decay_grad(1) + twice(
        lower,
        (twice(at_or_before, d_enter[2 * BLOCK :]) + twice(after, d_enter[BLOCK : 2 * BLOCK]))
        * tail1,
    )

    received(P_DN, R_DN, T2_DN, T3_DN)
    memory = (
        p_in[...].astype(F32)
        + prev1_fall1 * t_in[0].astype(F32)
        + (prev2_fall1 * prev1_all) * t_in[1].astype(F32)
    )
    middle_memory = own0 * memory + r_in[...].astype(F32) + u0c[...]
    m_in[...] = memory.astype(BF16)
    m_mid[...] = middle_memory.astype(BF16)
    fall_grad = jnp.concatenate(
        [
            own0 * jnp.sum(memory * mid_grad, axis=0, keepdims=True),
            own1 * jnp.sum(middle_memory * end_grad, axis=0, keepdims=True),
            jnp.zeros((6, WIDTH), F32),
        ],
        axis=0,
    )
    fall_grad = sum(nt(part, spread) for part in pieces(fall_grad, 2))
    received(DQ_DN)

    def query_step(pair, carry):
        at = lanes_of(pair)
        scaled = gq[:, at]
        carried = jnp.concatenate(
            [
                nt(scaled[:BLOCK], diagonal(m_in[:, at])),
                nt(scaled[BLOCK:], diagonal(m_mid[:, at])),
            ],
            axis=0,
        )
        xmat[pl.ds(4 * BLOCK, LANES), at] = (
            carried * qf[pl.ds(0, LANES), at].astype(F32)
        ).astype(BF16)
        coef = coef_ref[:, at]
        raw = q_ref[:, at].astype(F32)
        d_feat = (
            dqf[:, at]
            + carried
            + jnp.concatenate([dqn_in[:, at].astype(F32), jnp.zeros((BLOCK, LANES), F32)], axis=0)
        )
        dq_ref[:, at] = (d_feat * (0.125 + (0.25 * coef) * raw)).astype(BF16)
        coef_sum[0:1, at] = coef_sum[0:1, at] + jnp.sum(
            d_feat * (0.125 * raw * raw), axis=0, keepdims=True
        )
        return carry

    each_pair(query_step)
    d_out = nt(xmat[pl.ds(4 * BLOCK, LANES), :], spread)
    received(DA_DN)
    d_decay = jnp.concatenate(
        [
            d_decay0 + dan_in[...] + twice(upper_in, d_out[:BLOCK]) + fall_grad[0:1],
            d_decay1 + twice(upper_in, d_out[BLOCK:]) + fall_grad[1:2],
        ],
        axis=0,
    )
    is_decay = iota((LANES, LANES), 1) < HEADS
    d_logits = jnp.where(is_decay, -rate * sig * d_decay, d_gamma * gamma * (1.0 - sig))
    rates = jnp.sum(jnp.where(is_decay, -soft * d_decay, 0.0), axis=0, keepdims=True)
    d_hi, d_lo = pieces(d_logits, 2)
    gate = tn(d_hi, x) + tn(d_lo, x)

    def paired(rows):
        high = rows.astype(BF16).astype(F32)
        return jnp.concatenate([high, rows - high], axis=0).astype(BF16)

    no_rates = jnp.zeros((1, LANES), F32)
    for chunk in range(8):
        at = slice(chunk * LANES, (chunk + 1) * LANES)
        mine[chunk, 0:32, :] = gate[:32, at].astype(BF16)
        mine[chunk, 32:TALL, :] = paired(
            jnp.concatenate(
                [
                    coef_sum[0:1, at],
                    rates if chunk == 0 else no_rates,
                    jnp.zeros((6, LANES), F32),
                ],
                axis=0,
            )
        )

    def exchange(base, size, where, source, target):
        made = [
            pltpu.make_async_remote_copy(
                src_ref=source(hop),
                dst_ref=target,
                send_sem=sum_send.at[base + hop],
                recv_sem=sum_recv.at[base + hop],
                device_id=where(hop),
                device_id_type=MESH,
            )
            for hop in range(1, size)
        ]
        for one in made:
            one.start()
        return made

    def added(buffer, count):
        total = buffer[0].astype(F32)
        for index in range(1, count):
            total = total + buffer[index].astype(F32)
        return jnp.concatenate(
            [total[:32].astype(BF16), paired(total[32:40] + total[40:])], axis=0
        )

    made = exchange(0, 8, octet, lambda hop: mine.at[lax.rem(eight + hop, 8)], first.at[eight])
    first[eight] = mine[eight]
    dx_ref[...] = (nn(d_hi, w_hi) + (nn(d_hi, w_lo) + nn(d_lo, w_hi))).astype(BF16)
    for one in made:
        one.wait_recv()
    second[y] = added(first, 8)
    more = exchange(8, y_size, along_y, lambda hop: second.at[y], second.at[y])
    for one in more:
        one.wait_recv()
    made += more
    third[z] = added(second, y_size)
    more = exchange(8 + y_size, z_size, along_z, lambda hop: third.at[z], third.at[z])
    for one in more:
        one.wait_recv()
    made += more
    done[eight] = added(third, z_size)
    more = exchange(8 + y_size + z_size, 8, octet, lambda hop: done.at[eight], done.at[eight])
    for message in range(MESSAGES):
        sent(message)
    for one in more:
        one.wait_recv()
    made += more
    for chunk in range(8):
        at = slice(chunk * LANES, (chunk + 1) * LANES)
        total = done[chunk].astype(F32)
        gate_ref[:, at] = total[:32]
        rest = total[32:40] + total[40:]
        coef_out[:, at] = rest[0:1]
        if chunk == 0:
            rate_out[...] = rest[1:2, :HEADS]
    for one in made:
        one.wait_send()


def main_call(sizes, queries, keys, values, inputs, gate, coef, rate, cotangent):
    z_size, y_size = sizes
    rows = queries.shape[0]
    anywhere = pl.BlockSpec(memory_space=pltpu.HBM)
    block, full = (BLOCK, WIDTH), (LANES, WIDTH)
    out = jax.ShapeDtypeStruct((rows, WIDTH), BF16)
    tile = (TALL, LANES)
    scratch = [
        (full, BF16), (full, BF16), (full, BF16), (full, BF16), (full, BF16),
        (gate.shape, F32), (coef.shape, F32), (rate.shape, F32),
        (block, BF16), (block, BF16), ((3 * BLOCK, LANES), F32), ((8, LANES), F32), ((3, 8, LANES), F32),
        (block, BF16), (block, BF16), (block, BF16), ((2,) + block, BF16),
        (block, BF16), (block, BF16), (block, BF16), (block, BF16), (block, BF16), ((2,) + block, BF16),
        (block, BF16), (block, BF16), ((BLOCK, LANES), F32), ((BLOCK, LANES), F32),
        ((8, WIDTH), F32), ((3 * BLOCK, WIDTH), F32), (full, F32), ((4 * BLOCK, WIDTH), F32),
        (full, BF16), (full, BF16), (full, BF16),
        (block, F32), (block, F32), (block, F32),
        (block, BF16), (block, BF16), (block, BF16), (block, BF16), (block, BF16),
        (full, F32), (full, F32), (full, F32),
        ((3 * BLOCK, WIDTH), BF16), ((8 * BLOCK, WIDTH), BF16), ((8, WIDTH), F32),
        ((8,) + tile, BF16), ((8,) + tile, BF16), ((y_size,) + tile, BF16), ((z_size,) + tile, BF16),
        ((8,) + tile, BF16),
    ]
    count = 16 + y_size + z_size
    return pl.pallas_call(
        functools.partial(main_kernel, z_size, y_size),
        out_shape=[out, out, out, out]
        + [jax.ShapeDtypeStruct(a.shape, F32) for a in (gate, coef, rate)],
        in_specs=[anywhere] * 8,
        out_specs=[pl.BlockSpec(memory_space=pltpu.VMEM)] * 7,
        scratch_shapes=[pltpu.VMEM(shape, dtype) for shape, dtype in scratch]
        + [
            pltpu.SemaphoreType.DMA((number,))
            for number in (LOADS, MESSAGES, MESSAGES, count, count)
        ],
        compiler_params=pltpu.CompilerParams(
            collective_id=0, has_side_effects=True, vmem_limit_bytes=56 * 2**20
        ),
        name="window_backward",
    )(queries, keys, values, inputs, gate, coef, rate, cotangent)


def hand_out_kernel(*refs):
    count = 7
    sources, targets, sem = refs[:count], refs[count : 2 * count], refs[2 * count]
    copies = [
        pltpu.make_async_copy(source, target, sem.at[index])
        for index, (source, target) in enumerate(zip(sources, targets))
    ]
    for one in copies:
        one.start()
    for one in copies:
        one.wait()


def hand_out(results):
    anywhere = pl.BlockSpec(memory_space=pltpu.HBM)
    return pl.pallas_call(
        hand_out_kernel,
        out_shape=[jax.ShapeDtypeStruct(a.shape, a.dtype) for a in results],
        in_specs=[pl.BlockSpec(memory_space=pltpu.VMEM)] * len(results),
        out_specs=[anywhere] * len(results),
        scratch_shapes=[pltpu.SemaphoreType.DMA((len(results),))],
        name="hand_out",
    )(*results)


def on_device(sizes, queries, keys, values, inputs, gate, coef, rate, cotangent):
    results = main_call(
        sizes,
        queries[0], keys[0], values[0], inputs[0], gate.T, coef[None], rate[None], cotangent[0],
    )
    dq, dk, dv, dx, d_gate, d_coef, d_rate = hand_out(results)
    return (dq[None], dk[None], dv[None], dx[None], d_gate.T, d_coef[0], d_rate[0])


def solution(mesh):
    rows = P("dp", "seq", None)
    y_size = min(4, max(1, mesh.shape["dp"] // 2))
    sizes = (mesh.shape["dp"] // (2 * y_size), y_size)
    return jax.shard_map(
        functools.partial(on_device, sizes),
        mesh=mesh,
        in_specs=(rows, rows, rows, rows, P(), P(), P(), rows),
        out_specs=(rows, rows, rows, rows, P(), P(), P()),
        check_vma=False,
    )
```

time: 66 us -> 50.8 us (0.77)
  local copies, waits for them, and re-layouts: 10.9 us -> 0 us
  Pallas kernels: 54.1 us -> 50.1 us
    unnamed x20 -> x0, local copies, waits for them, and re-layouts: 9.13 us -> none
    pallas_call x2, Pallas kernels: 54.1 us -> 50.1 us  [the longest x1 47.8 us: main_call(): pl.pallas_call(functools.partial(main_kernel, z_size, y_size), out_shape=...]
    transpose x1 -> x0, local copies, waits for them, and re-layouts: 0.66 us -> none  [on_device(): total[:32]]
where the time goes in v2:
time: 50.8 us; the launch traced here: 50.7 us
  Pallas kernels  50.1 us (99%)
  between operations  0.64 us (1%)
    pallas_call x1, Pallas kernels, main_call(): pl.pallas_call(functools.partial(main_kernel, z_size, y_size), out_shape=...  47.8 us
    pallas_call x1, Pallas kernels, hand_out(): pl.pallas_call(hand_out_kernel, out_shape=[jax.ShapeDtypeStruct(a.shape,...  2.29 us

profile of v2, /device:TPU:1, one launch (start us, length us, event | category | flops | bytes accessed | tf_op | source)
XLA Modules:
  0.0 50.7 jit_solution(15451833976930581024)
XLA Ops:
  0.6 47.8 %window_backward.1 = (bf16[128,1024]{1,0:T(8,128)(2,1)}, bf16[128,1024]{1,0:T(8,128)(2,1)}, bf16[128,1024]{1,0:T(8,128)(2,1)}, bf16[128,1024]{1,0:T(8,128)(2,1)}...) custom-call(bf16[128,1024]{1,0:T(8,128)(2,1)} %bitcast.15, bf16[128,1024]{1,0:T(8,128)(2,1)} %bitcast.16, ...), custom_call_target="tpu_custom_call" | custom-call | tf_op jit(solution)/shard_map/window_backward/pallas_call | solution.py:648
  48.4 2.3 %hand_out.1 = (bf16[128,1024]{1,0:T(8,128)(2,1)}, bf16[128,1024]{1,0:T(8,128)(2,1)}, bf16[128,1024]{1,0:T(8,128)(2,1)}, bf16[128,1024]{1,0:T(8,128)(2,1)}, f32[3...) custom-call(bf16[128,1024]{1,0:T(8,128)(2,1)} %get-tuple-element.21.refs_0_, ...), custom_call_target="tpu_custom_call" | custom-call | tf_op jit(solution)/shard_map/hand_out/pallas_call | solution.py:681

commit v3 on v2

--- a/solution.py
+++ b/solution.py
@@ -50,20 +50,23 @@
 P_DN, R_DN, T2_DN, T3_DN, DQ_DN, DA_DN = range(9, 15)
 MESSAGES = 15
 LOADS = 8
+STORES = 5
 TALL = 48
+NEVER = -1e30
 
 
 def main_kernel(
     z_size, y_size,
     q_hbm, k_hbm, v_hbm, x_hbm, w_hbm, coef_hbm, rate_hbm, g_hbm,
-    dq_ref, dk_ref, dv_ref, dx_ref, gate_ref, coef_out, rate_out,
+    dq_hbm, dk_hbm, dv_hbm, dx_hbm, done_hbm,
     q_ref, k_ref, v_ref, x_ref, g_ref, w_ref, coef_ref, rate_ref,
+    dq_ref, dk_ref, dv_ref, dx_ref,
     qn, gn, lbuf, tot, tot_in, s1_out, ss_out, s1_in, ss_in, p_out, r_out, t_out, p_in, r_in, t_in,
     dqn_out, dqn_in, dan_out, dan_in,
     lrow, lx, gamma_x, blast_x, qf, wk, gq, s1c, u0c, c1c, m_in, m_mid, n_mid, n_end, z_end,
     dqf, dwk, dvf, gmat, xmat, coef_sum,
     mine, first, second, third, done,
-    load_sem, send_sem, recv_sem, sum_send, sum_recv,
+    load_sem, store_sem, send_sem, recv_sem, sum_send, sum_recv,
 ):
     place, dp = lax.axis_index("seq"), lax.axis_index("dp")
     z, y, core = dp // (y_size * 2), (dp // 2) % y_size, dp % 2
@@ -80,6 +83,13 @@
     ]
     for load in loads:
         load.start()
+    stores = [
+        pltpu.make_async_copy(source, target, store_sem.at[index])
+        for index, (source, target) in enumerate(
+            ((dq_ref, dq_hbm), (dk_ref, dk_hbm), (dv_ref, dv_hbm), (dx_ref, dx_hbm))
+        )
+    ]
+
     def copy(source, target, message, to):
         return pltpu.make_async_remote_copy(
             src_ref=source,
@@ -182,6 +192,8 @@
     head_lane = iota((LANES, WIDTH), 1) // BLOCK
     spread = flag(head_row == head_lane)
     spread_gate = flag(head_row == head_lane + HEADS)
+    spread_pieces = flag(head_row % 32 == head_lane)
+    head_lanes = iota((BLOCK, LANES), 1) < HEADS
     left = iota((BLOCK, LANES), 1) < BLOCK
     left1 = iota((1, LANES), 1) < BLOCK
     srow, scol = iota((BLOCK, BLOCK), 0), iota((BLOCK, BLOCK), 1)
@@ -193,11 +205,11 @@
     loads[0].wait()
     loads[1].wait()
     loads[2].wait()
-    w_hi, w_lo = pieces(
-        jnp.concatenate([w_ref[...], jnp.zeros((LANES - 2 * HEADS, WIDTH), F32)], axis=0), 2
-    )
+    w_hi, w_lo = pieces(w_ref[...], 2)
+    no_rows = jnp.zeros((32, WIDTH), BF16)
     x = x_ref[...]
-    logits = nt(x, w_hi) + nt(x, w_lo)
+    logits = nt(x, jnp.concatenate([w_hi, no_rows, w_lo, no_rows], axis=0))
+    logits = logits + jnp.concatenate([logits[:, BLOCK:], logits[:, :BLOCK]], axis=1)
     small = jnp.exp(-jnp.abs(logits))
     soft = jnp.maximum(logits, 0.0) + jnp.log1p(small)
     sig = jnp.where(logits >= 0.0, 1.0, small) / (1.0 + small)
@@ -210,8 +222,17 @@
     tot[0:1, :] = log_own[BLOCK - 1 : BLOCK]
     tot[1:2, :] = log_own[LANES - 1 :]
 
-    def expand(a, count):
-        return sum(nn(part, spread) for part in pieces(a, count))
+    for load in loads[3:]:
+        load.wait()
+    pl.semaphore_wait(barrier, partners)
+    send(L_UP, TOT1, TOT2, TOT3, Q_UP, G_UP)
+
+    def beside(a):
+        parts = [part[:, :32] for part in pieces(a, 3)]
+        return jnp.concatenate(parts + [jnp.zeros((a.shape[0], 32), BF16)], axis=1)
+
+    def expand(a):
+        return nn(beside(a), spread_pieces)
 
     def block_rows(logs, block, offset):
         pick = flag(row == (col % BLOCK) + offset)
@@ -221,21 +242,30 @@
                 left1, turned[2 * pair : 2 * pair + 1], turned[2 * pair + 1 : 2 * pair + 2]
             )
 
-    lx[pl.ds(0, LANES), :] = expand(log_own, 3)
-    gamma_x[...] = sum(nn(part, spread_gate) for part in pieces(gamma, 2))
-
     tail0 = jnp.exp(log_own[BLOCK - 1 : BLOCK] - log_own[:BLOCK])
     tail1 = jnp.exp(log_own[LANES - 1 :] - log_own[BLOCK:])
 
+    def twice(mask, a):
+        return nn(
+            jnp.concatenate([mask, mask], axis=1), jnp.concatenate(pieces(a, 2), axis=0)
+        )
+
     def ending(mask, tail):
-        return expand(sum(nn(mask, part) for part in pieces(tail, 2)), 2)
-
-    blast_x[pl.ds(0, BLOCK), :] = ending(upper_in, tail0)
-    blast_x[pl.ds(BLOCK, BLOCK), :] = ending(lower, tail1)
-    blast_x[pl.ds(2 * BLOCK, BLOCK), :] = ending(upper_in, tail1)
-
-    def each_pair(step):
-        lax.fori_loop(0, PAIRS, step, 0, unroll=PAIRS)
+        return jnp.where(head_lanes, twice(mask, tail), 0.0)
+
+    gamma_first = jnp.concatenate([gamma[:, HEADS:32], jnp.zeros((LANES, LANES - HEADS), F32)], axis=1)
+    expanded = expand(
+        jnp.concatenate(
+            [log_own, gamma_first, ending(upper_in, tail0), ending(lower, tail1), ending(upper_in, tail1)],
+            axis=0,
+        )
+    )
+    lx[pl.ds(0, LANES), :] = expanded[:LANES]
+    gamma_x[...] = expanded[LANES : 2 * LANES]
+    blast_x[pl.ds(0, 3 * BLOCK), :] = expanded[2 * LANES :]
+
+    def each_pair(step, begin=0, end=PAIRS):
+        lax.fori_loop(begin, end, step, 0, unroll=end - begin)
 
     def lanes_of(pair):
         return pl.ds(pl.multiple_of(pair * LANES, LANES), LANES)
@@ -253,9 +283,6 @@
 
     def weighted(a, weights):
         return (a.astype(F32) * weights).astype(BF16)
-
-    for load in loads[3:]:
-        load.wait()
 
     def own_step(pair, carry):
         at = lanes_of(pair)
@@ -286,8 +313,7 @@
         return carry
 
     each_pair(own_step)
-    pl.semaphore_wait(barrier, partners)
-    send(L_UP, TOT1, TOT2, TOT3, Q_UP, G_UP, S_UP, SS2_UP, SS3_UP, P_DN)
+    send(S_UP, SS2_UP, SS3_UP, P_DN)
 
     block_rows(log_own, 0, 0)
     block_rows(log_own, 1, BLOCK)
@@ -305,7 +331,7 @@
 
     def tile(keys_bd, values_bd, queries, grads, kernel):
         scores = nt(queries, keys_bd)
-        d_weights = nt(grads, values_bd).astype(BF16).astype(F32)
+        d_weights = nt(grads, values_bd)
         weights = (scores * kernel).astype(BF16)
         d_scores = (d_weights * kernel).astype(BF16)
         d_kernel = (d_weights * scores).astype(BF16)
@@ -323,8 +349,7 @@
         rows = jnp.concatenate(
             [jnp.broadcast_to(lrow[b : b + 1, at], (BLOCK, LANES)) for b in range(2)], axis=0
         )
-        gaps = jnp.where(causal, lx[pl.ds(0, LANES), at] - rows, 0.0)
-        decays = jnp.where(causal, jnp.exp(gaps), 0.0)
+        decays = jnp.exp(jnp.where(causal, lx[pl.ds(0, LANES), at] - rows, NEVER))
         low = decays.astype(BF16)
         start = nn(low[:BLOCK], cur_mask)
         middle = nn(low[BLOCK:], both_mask)
@@ -352,11 +377,14 @@
         gmat[pl.ds(0, LANES), at] = (d_decays * decays).astype(BF16)
         return carry
 
+    each_pair(window_step, 0, 3)
+
     received(L_UP)
     log_next = lbuf[pl.ds(2 * BLOCK, BLOCK), :]
-    lx[pl.ds(LANES, BLOCK), :] = expand(log_next, 3)
     tail2 = jnp.exp(log_next[BLOCK - 1 :] - log_next)
-    blast_x[pl.ds(3 * BLOCK, BLOCK), :] = ending(lower, tail2)
+    expanded = expand(jnp.concatenate([log_next, ending(lower, tail2)], axis=0))
+    lx[pl.ds(LANES, BLOCK), :] = expanded[:BLOCK]
+    blast_x[pl.ds(3 * BLOCK, BLOCK), :] = expanded[BLOCK:]
 
     def next_step(pair, carry):
         at = lanes_of(pair)
@@ -370,7 +398,7 @@
     each_pair(next_step)
     send(T2_DN, T3_DN, R_DN)
 
-    each_pair(window_step)
+    each_pair(window_step, 3, PAIRS)
     block_rows(lbuf[pl.ds(BLOCK, LANES), :], 2, BLOCK)
 
     received(Q_UP, G_UP)
@@ -381,12 +409,14 @@
         grads = gn[:, at]
         logs = lx[pl.ds(LANES, BLOCK), at]
         held = causal[:BLOCK]
-        decays = jnp.where(held, jnp.exp(jnp.where(held, logs - lrow[2:3, at], 0.0)), 0.0)
+        decays = jnp.exp(jnp.where(held, logs - lrow[2:3, at], NEVER))
         dq, dv, dk, db = tile(
             diagonal(wk[pl.ds(BLOCK, BLOCK), at]), diagonal(v_ref[pl.ds(BLOCK, BLOCK), at]),
             queries, grads, nn(decays.astype(BF16), prev_mask),
         )
         dqn_out[:, at] = dq.astype(BF16)
+        raw = qn[:, at].astype(F32)
+        coef_sum[1:2, at] = jnp.sum(dq * (0.125 * raw * raw), axis=0, keepdims=True)
         dvf[pl.ds(BLOCK, BLOCK), at] = dvf[pl.ds(BLOCK, BLOCK), at] + dv
         dwk[pl.ds(BLOCK, BLOCK), at] = dwk[pl.ds(BLOCK, BLOCK), at] + dk
         gmat[pl.ds(LANES, BLOCK), at] = (nt(db, prev_mask) * decays).astype(BF16)
@@ -400,13 +430,11 @@
         later = nn(upper_in, gmat[pl.ds(block * BLOCK, BLOCK), :])
         lanes = iota((BLOCK, WIDTH), 1) % BLOCK
         kept = jnp.where(lanes < iota((BLOCK, WIDTH), 0), later, 0.0)
-        return sum(nt(part, spread) for part in pieces(kept, 2))
-
-    def twice(mask, a):
-        return sum(nn(mask, part) for part in pieces(a, 2))
+        return nt(kept.astype(BF16), spread)
 
     received(TOT1, S_UP, TOT2, SS2_UP, SS3_UP, TOT3)
-    falls = [expand(tot_in[slot], 3) for slot in range(3)]
+    falls = expand(jnp.concatenate([tot_in[slot] for slot in range(3)], axis=0))
+    falls = [falls[8 * slot : 8 * slot + 8] for slot in range(3)]
     next1_fall1 = jnp.exp(falls[0][1:2])
     next2_all = jnp.exp(falls[1][0:1] + falls[1][1:2])
     prev1_fall1 = jnp.exp(falls[2][1:2])
@@ -427,7 +455,6 @@
     def enter(index, keys, d_role, at):
         weights = blast_x[pl.ds(index * BLOCK, BLOCK), at]
         own_keys = keys.astype(F32)
-        d_role = d_role.astype(BF16).astype(F32)
         xmat[pl.ds(index * BLOCK, BLOCK), at] = (d_role * own_keys).astype(BF16)
         return (own_keys * weights).astype(BF16), d_role * weights
 
@@ -471,16 +498,16 @@
         return carry
 
     each_pair(inner_step)
+    stores[1].start()
+    stores[2].start()
     d_enter = nt(xmat[pl.ds(0, 3 * BLOCK), :], spread)
-    d_gate = nt(xmat[pl.ds(6 * BLOCK, LANES), :], spread)
-    shift = flag(col == row + HEADS)
-    d_gamma = sum(nn(part, shift) for part in pieces(d_gate, 2))
+    d_gamma = nt(xmat[pl.ds(6 * BLOCK, LANES), :], spread_gate)
     d_decay0 = decay_grad(0) + twice(lower, twice(at_or_before, d_enter[:BLOCK]) * tail0)
-    d_decay1 = decay_grad(1) + twice(
-        lower,
-        (twice(at_or_before, d_enter[2 * BLOCK :]) + twice(after, d_enter[BLOCK : 2 * BLOCK]))
-        * tail1,
-    )
+    entered = nn(
+        jnp.concatenate([at_or_before, at_or_before, after, after], axis=1),
+        jnp.concatenate(pieces(d_enter[2 * BLOCK :], 2) + pieces(d_enter[BLOCK : 2 * BLOCK], 2), axis=0),
+    )
+    d_decay1 = decay_grad(1) + twice(lower, entered * tail1)
 
     received(P_DN, R_DN, T2_DN, T3_DN)
     memory = (
@@ -500,7 +527,6 @@
         axis=0,
     )
     fall_grad = sum(nt(part, spread) for part in pieces(fall_grad, 2))
-    received(DQ_DN)
 
     def query_step(pair, carry):
         at = lanes_of(pair)
@@ -515,16 +541,13 @@
         xmat[pl.ds(4 * BLOCK, LANES), at] = (
             carried * qf[pl.ds(0, LANES), at].astype(F32)
         ).astype(BF16)
-        coef = coef_ref[:, at]
         raw = q_ref[:, at].astype(F32)
-        d_feat = (
-            dqf[:, at]
-            + carried
-            + jnp.concatenate([dqn_in[:, at].astype(F32), jnp.zeros((BLOCK, LANES), F32)], axis=0)
-        )
-        dq_ref[:, at] = (d_feat * (0.125 + (0.25 * coef) * raw)).astype(BF16)
-        coef_sum[0:1, at] = coef_sum[0:1, at] + jnp.sum(
-            d_feat * (0.125 * raw * raw), axis=0, keepdims=True
+        d_feat = dqf[:, at] + carried
+        dqf[:, at] = d_feat
+        coef_sum[0:1, at] = (
+            coef_sum[0:1, at]
+            + coef_sum[1:2, at]
+            + jnp.sum(d_feat * (0.125 * raw * raw), axis=0, keepdims=True)
         )
         return carry
 
@@ -541,8 +564,8 @@
     is_decay = iota((LANES, LANES), 1) < HEADS
     d_logits = jnp.where(is_decay, -rate * sig * d_decay, d_gamma * gamma * (1.0 - sig))
     rates = jnp.sum(jnp.where(is_decay, -soft * d_decay, 0.0), axis=0, keepdims=True)
-    d_hi, d_lo = pieces(d_logits, 2)
-    gate = tn(d_hi, x) + tn(d_lo, x)
+    gate = nn(jnp.concatenate(pieces(d_logits.T[:32], 2), axis=0), x)
+    gate = gate[:32] + gate[32:]
 
     def paired(rows):
         high = rows.astype(BF16).astype(F32)
@@ -563,7 +586,7 @@
             )
         )
 
-    def exchange(base, size, where, source, target):
+    def exchange(base, size, where, source, target, reach=1):
         made = [
             pltpu.make_async_remote_copy(
                 src_ref=source(hop),
@@ -573,7 +596,7 @@
                 device_id=where(hop),
                 device_id_type=MESH,
             )
-            for hop in range(1, size)
+            for hop in sorted(range(1, size), key=lambda hop: -min(hop // reach, (size - hop) // reach))
         ]
         for one in made:
             one.start()
@@ -587,9 +610,27 @@
             [total[:32].astype(BF16), paired(total[32:40] + total[40:])], axis=0
         )
 
-    made = exchange(0, 8, octet, lambda hop: mine.at[lax.rem(eight + hop, 8)], first.at[eight])
+    made = exchange(0, 8, octet, lambda hop: mine.at[lax.rem(eight + hop, 8)], first.at[eight], 2)
     first[eight] = mine[eight]
-    dx_ref[...] = (nn(d_hi, w_hi) + (nn(d_hi, w_lo) + nn(d_lo, w_hi))).astype(BF16)
+    d_hi, d_lo = [part[:, :32] for part in pieces(d_logits, 2)]
+    dx_ref[...] = nn(
+        jnp.concatenate([d_hi, d_lo, d_hi, jnp.zeros((LANES, 32), BF16)], axis=1),
+        jnp.concatenate([w_hi, w_hi, w_lo, no_rows], axis=0),
+    ).astype(BF16)
+    stores[3].start()
+    received(DQ_DN)
+
+    def last_step(pair, carry):
+        at = lanes_of(pair)
+        raw = q_ref[:, at].astype(F32)
+        d_feat = dqf[:, at] + jnp.concatenate(
+            [dqn_in[:, at].astype(F32), jnp.zeros((BLOCK, LANES), F32)], axis=0
+        )
+        dq_ref[:, at] = (d_feat * (0.125 + (0.25 * coef_ref[:, at]) * raw)).astype(BF16)
+        return carry
+
+    each_pair(last_step)
+    stores[0].start()
     for one in made:
         one.wait_recv()
     second[y] = added(first, 8)
@@ -602,23 +643,21 @@
     for one in more:
         one.wait_recv()
     made += more
-    done[eight] = added(third, z_size)
-    more = exchange(8 + y_size + z_size, 8, octet, lambda hop: done.at[eight], done.at[eight])
+    done[...] = added(third, z_size)
+    own = pltpu.make_async_copy(done, done_hbm.at[eight], store_sem.at[4])
+    own.start()
+    more = exchange(
+        8 + y_size + z_size, 8, octet, lambda hop: done, done_hbm.at[eight], 2
+    )
     for message in range(MESSAGES):
         sent(message)
-    for one in more:
-        one.wait_recv()
-    made += more
-    for chunk in range(8):
-        at = slice(chunk * LANES, (chunk + 1) * LANES)
-        total = done[chunk].astype(F32)
-        gate_ref[:, at] = total[:32]
-        rest = total[32:40] + total[40:]
-        coef_out[:, at] = rest[0:1]
-        if chunk == 0:
-            rate_out[...] = rest[1:2, :HEADS]
+    for store in stores:
+        store.wait()
+    own.wait()
     for one in made:
         one.wait_send()
+    for one in more:
+        one.wait()
 
 
 def main_call(sizes, queries, keys, values, inputs, gate, coef, rate, cotangent):
@@ -631,6 +670,7 @@
     scratch = [
         (full, BF16), (full, BF16), (full, BF16), (full, BF16), (full, BF16),
         (gate.shape, F32), (coef.shape, F32), (rate.shape, F32),
+        (full, BF16), (full, BF16), (full, BF16), (full, BF16),
         (block, BF16), (block, BF16), ((3 * BLOCK, LANES), F32), ((8, LANES), F32), ((3, 8, LANES), F32),
         (block, BF16), (block, BF16), (block, BF16), ((2,) + block, BF16),
         (block, BF16), (block, BF16), (block, BF16), (block, BF16), (block, BF16), ((2,) + block, BF16),
@@ -642,19 +682,18 @@
         (full, F32), (full, F32), (full, F32),
         ((3 * BLOCK, WIDTH), BF16), ((8 * BLOCK, WIDTH), BF16), ((8, WIDTH), F32),
         ((8,) + tile, BF16), ((8,) + tile, BF16), ((y_size,) + tile, BF16), ((z_size,) + tile, BF16),
-        ((8,) + tile, BF16),
+        (tile, BF16),
     ]
     count = 16 + y_size + z_size
     return pl.pallas_call(
         functools.partial(main_kernel, z_size, y_size),
-        out_shape=[out, out, out, out]
-        + [jax.ShapeDtypeStruct(a.shape, F32) for a in (gate, coef, rate)],
+        out_shape=[out, out, out, out, jax.ShapeDtypeStruct((8,) + tile, BF16)],
         in_specs=[anywhere] * 8,
-        out_specs=[pl.BlockSpec(memory_space=pltpu.VMEM)] * 7,
+        out_specs=[anywhere] * 5,
         scratch_shapes=[pltpu.VMEM(shape, dtype) for shape, dtype in scratch]
         + [
             pltpu.SemaphoreType.DMA((number,))
-            for number in (LOADS, MESSAGES, MESSAGES, count, count)
+            for number in (LOADS, STORES, MESSAGES, MESSAGES, count, count)
         ],
         compiler_params=pltpu.CompilerParams(
             collective_id=0, has_side_effects=True, vmem_limit_bytes=56 * 2**20
@@ -664,26 +703,48 @@
 
 
 def hand_out_kernel(*refs):
-    count = 7
-    sources, targets, sem = refs[:count], refs[count : 2 * count], refs[2 * count]
-    copies = [
-        pltpu.make_async_copy(source, target, sem.at[index])
-        for index, (source, target) in enumerate(zip(sources, targets))
+    sources, targets, held = refs[:5], refs[5:12], refs[12:20]
+    load_sem, store_sem = refs[20:]
+    loads = [
+        pltpu.make_async_copy(sources[index], held[index], load_sem.at[index]) for index in range(5)
     ]
-    for one in copies:
-        one.start()
-    for one in copies:
-        one.wait()
+    stores = [
+        pltpu.make_async_copy(held[index if index < 4 else index + 1], targets[index], store_sem.at[index])
+        for index in range(7)
+    ]
+    for load in loads[::-1]:
+        load.start()
+    done, gate, coef, rate = held[4:]
+    loads[4].wait()
+    for chunk in range(8):
+        at = slice(chunk * LANES, (chunk + 1) * LANES)
+        total = done[chunk].astype(F32)
+        gate[:, at] = total[:32]
+        rest = total[32:40] + total[40:]
+        coef[:, at] = rest[0:1]
+        if chunk == 0:
+            rate[...] = rest[1:2, :HEADS]
+    for store in stores[4:]:
+        store.start()
+    for index in range(3, -1, -1):
+        loads[index].wait()
+        stores[index].start()
+    for store in stores:
+        store.wait()
 
 
 def hand_out(results):
     anywhere = pl.BlockSpec(memory_space=pltpu.HBM)
+    params = [jax.ShapeDtypeStruct(shape, F32) for shape in ((32, WIDTH), (1, WIDTH), (1, HEADS))]
+    shapes = [jax.ShapeDtypeStruct(a.shape, a.dtype) for a in results]
     return pl.pallas_call(
         hand_out_kernel,
-        out_shape=[jax.ShapeDtypeStruct(a.shape, a.dtype) for a in results],
-        in_specs=[pl.BlockSpec(memory_space=pltpu.VMEM)] * len(results),
-        out_specs=[anywhere] * len(results),
-        scratch_shapes=[pltpu.SemaphoreType.DMA((len(results),))],
+        out_shape=shapes[:4] + params,
+        in_specs=[anywhere] * 5,
+        out_specs=[anywhere] * 7,
+        scratch_shapes=[pltpu.VMEM(a.shape, a.dtype) for a in shapes + params]
+        + [pltpu.SemaphoreType.DMA((5,)), pltpu.SemaphoreType.DMA((7,))],
+        compiler_params=pltpu.CompilerParams(vmem_limit_bytes=56 * 2**20),
         name="hand_out",
     )(*results)
 

time: 50.8 us -> 47.7 us (0.939)
  Pallas kernels: 50.1 us -> 47 us
    pallas_call x1, Pallas kernels: 47.8 us -> 44.9 us  [main_call(): pl.pallas_call(functools.partial(main_kernel, z_size, y_size), out_shape=...]
where the time goes in v3:
time: 47.7 us; the launch traced here: 47.6 us
  Pallas kernels  47 us (99%)
  between operations  0.64 us (1%)
    pallas_call x1, Pallas kernels, main_call(): pl.pallas_call(functools.partial(main_kernel, z_size, y_size), out_shape=...  44.9 us
    pallas_call x1, Pallas kernels, hand_out(): pl.pallas_call(hand_out_kernel, out_shape=shapes[:4] + params, in_specs=[...  2.08 us

profile of v3, /device:TPU:1, one launch (start us, length us, event | category | flops | bytes accessed | tf_op | source)
XLA Modules:
  0.0 47.6 jit_solution(6259719466500785738)
XLA Ops:
  0.6 44.9 %window_backward.1 = (bf16[128,1024]{1,0:T(8,128)(2,1)}, bf16[128,1024]{1,0:T(8,128)(2,1)}, bf16[128,1024]{1,0:T(8,128)(2,1)}, bf16[128,1024]{1,0:T(8,128)(2,1)}, bf16[8,48,128]{2,1,0:T(8,128)(2,1)}) custom-call(bf16[128,1024]{1,0:T(8,128)(2,1)} %bitcast.15, bf16[128,1024]{1,0:T(8,128)(2,1)} %bitcast.16, bf16[128,1024]{1,0:T(8,128)(2,1)} %bitcast.17, ...), custom_call_target="tpu_custom_call" | custom-call | tf_op jit(solution)/shard_map/window_backward/pallas_call | solution.py:688
  45.5 2.1 %hand_out.1 = (bf16[128,1024]{1,0:T(8,128)(2,1)}, bf16[128,1024]{1,0:T(8,128)(2,1)}, bf16[128,1024]{1,0:T(8,128)(2,1)}, bf16[128,1024]{1,0:T(8,128)(2,1)}, f32[3...) custom-call(bf16[128,1024]{1,0:T(8,128)(2,1)} %get-tuple-element.19.refs_0_, ...), custom_call_target="tpu_custom_call" | custom-call | tf_op jit(solution)/shard_map/hand_out/pallas_call | solution.py:740

commit v4 on v3

--- a/solution.py
+++ b/solution.py
@@ -46,9 +46,9 @@
     return lax.broadcasted_iota(jnp.int32, shape, dimension)
 
 
-Q_UP, G_UP, L_UP, S_UP, SS2_UP, SS3_UP, TOT1, TOT2, TOT3 = range(9)
-P_DN, R_DN, T2_DN, T3_DN, DQ_DN, DA_DN = range(9, 15)
-MESSAGES = 15
+Q_UP, G_UP, L_UP, S_UP, SS1_UP, SS2_UP, SS3_UP, TOT1, TOT2, TOT3 = range(10)
+P_DN, R_DN, T2_DN, T3_DN, DQ_DN, DA_DN = range(10, 16)
+MESSAGES = 16
 LOADS = 8
 STORES = 5
 TALL = 48
@@ -61,12 +61,12 @@
     dq_hbm, dk_hbm, dv_hbm, dx_hbm, done_hbm,
     q_ref, k_ref, v_ref, x_ref, g_ref, w_ref, coef_ref, rate_ref,
     dq_ref, dk_ref, dv_ref, dx_ref,
-    qn, gn, lbuf, tot, tot_in, s1_out, ss_out, s1_in, ss_in, p_out, r_out, t_out, p_in, r_in, t_in,
+    qn, gn, lbuf, tot, tot_in, s1_out, ss_out, s1_in, ss_held, ss_in, p_out, r_out, t_out, p_in, r_in, t_in,
     dqn_out, dqn_in, dan_out, dan_in,
     lrow, lx, gamma_x, blast_x, qf, wk, gq, s1c, u0c, c1c, m_in, m_mid, n_mid, n_end, z_end,
     dqf, dwk, dvf, gmat, xmat, coef_sum,
     mine, first, second, third, done,
-    load_sem, store_sem, send_sem, recv_sem, sum_send, sum_recv,
+    load_sem, store_sem, send_sem, recv_sem, sum_send, sum_recv, ring_sem,
 ):
     place, dp = lax.axis_index("seq"), lax.axis_index("dp")
     z, y, core = dp // (y_size * 2), (dp // 2) % y_size, dp % 2
@@ -103,45 +103,42 @@
     up1, up2, up3 = place - 1, place - 2, place - 3
     dn1, dn2, dn3 = place + 1, place + 2, place + 3
     around = [lax.rem(place + 4 - hop, 4) for hop in (1, 2, 3)]
-    copies = {
-        Q_UP: (copy(q_ref.at[pl.ds(0, BLOCK)], qn, Q_UP, up1), 1),
-        G_UP: (copy(g_ref.at[pl.ds(0, BLOCK)], gn, G_UP, up1), 1),
-        L_UP: (copy(lbuf.at[pl.ds(0, BLOCK)], lbuf.at[pl.ds(2 * BLOCK, BLOCK)], L_UP, up1), 1),
-        S_UP: (copy(s1_out, s1_in, S_UP, up1), 1),
-        SS2_UP: (copy(ss_out, ss_in.at[0], SS2_UP, up2), 2),
-        SS3_UP: (copy(ss_out, ss_in.at[1], SS3_UP, up3), 3),
-        TOT1: (copy(tot, tot_in.at[0], TOT1, around[0]), 0),
-        TOT2: (copy(tot, tot_in.at[1], TOT2, around[1]), 0),
-        TOT3: (copy(tot, tot_in.at[2], TOT3, around[2]), 0),
-        P_DN: (copy(p_out, p_in, P_DN, dn1), -1),
-        R_DN: (copy(r_out, r_in, R_DN, dn1), -1),
-        T2_DN: (copy(t_out, t_in.at[0], T2_DN, dn2), -2),
-        T3_DN: (copy(t_out, t_in.at[1], T3_DN, dn3), -3),
-        DQ_DN: (copy(dqn_out, dqn_in, DQ_DN, dn1), -1),
-        DA_DN: (copy(dan_out, dan_in, DA_DN, dn1), -1),
+    always = place >= 0
+    later, earlier = place >= 1, place < last
+    messages = {
+        Q_UP: (copy(q_ref.at[pl.ds(0, BLOCK)], qn, Q_UP, up1), later, earlier),
+        G_UP: (copy(g_ref.at[pl.ds(0, BLOCK)], gn, G_UP, up1), later, earlier),
+        L_UP: (
+            copy(lbuf.at[pl.ds(0, BLOCK)], lbuf.at[pl.ds(2 * BLOCK, BLOCK)], L_UP, up1), later, earlier
+        ),
+        S_UP: (copy(s1_out, s1_in, S_UP, up1), later, earlier),
+        SS1_UP: (copy(ss_out, ss_held, SS1_UP, up1), place == 3, place == 2),
+        SS2_UP: (copy(ss_out, ss_in.at[0], SS2_UP, up2), place == 2, place == 0),
+        SS3_UP: (copy(ss_out, ss_in.at[1], SS3_UP, up3), place == 3, place == 0),
+        TOT1: (copy(tot, tot_in.at[0], TOT1, around[0]), always, always),
+        TOT2: (copy(tot, tot_in.at[1], TOT2, around[1]), always, always),
+        TOT3: (copy(tot, tot_in.at[2], TOT3, around[2]), always, always),
+        P_DN: (copy(p_out, p_in, P_DN, dn1), earlier, later),
+        R_DN: (copy(r_out, r_in, R_DN, dn1), earlier, later),
+        T2_DN: (copy(t_out, t_in.at[0], T2_DN, dn2), place == 1, place == 3),
+        T3_DN: (copy(t_out, t_in.at[1], T3_DN, dn3), place == 0, place == 3),
+        DQ_DN: (copy(dqn_out, dqn_in, DQ_DN, dn1), earlier, later),
+        DA_DN: (copy(dan_out, dan_in, DA_DN, dn1), earlier, later),
     }
 
-    def guarded(steps, action):
-        if steps == 0:
-            action()
-        elif steps > 0:
-            pl.when(place >= steps)(action)
-        else:
-            pl.when(place <= last + steps)(action)
-
-    def send(*messages):
-        for message in messages:
-            description, steps = copies[message]
-            guarded(steps, description.start)
+    def send(*which, places=always):
+        for message in which:
+            description, senders, _ = messages[message]
+            pl.when(senders & places)(description.start)
 
     def sent(message):
-        description, steps = copies[message]
-        guarded(steps, description.wait_send)
-
-    def received(*messages):
-        for message in messages:
-            description, steps = copies[message]
-            guarded(-steps, description.wait_recv)
+        description, senders, _ = messages[message]
+        pl.when(senders)(description.wait_send)
+
+    def received(*which, places=always):
+        for message in which:
+            description, _, getters = messages[message]
+            pl.when(getters & places)(description.wait_recv)
 
     eight = place * 2 + core
 
@@ -157,10 +154,20 @@
 
     barrier = pltpu.get_barrier_semaphore()
     partners = 0
-    for where, size in ((octet, 8), (along_y, y_size), (along_z, z_size)):
-        for hop in range(1, size):
+    ring = z_size == 8
+    near = (1, z_size - 1) if ring else range(1, z_size)
+    for where, hops in ((octet, range(1, 8)), (along_y, range(1, y_size)), (along_z, near)):
+        for hop in hops:
             pl.semaphore_signal(barrier, inc=1, device_id=where(hop), device_id_type=MESH)
             partners += 1
+
+    def tell(index, hop):
+        if ring:
+            pl.semaphore_signal(ring_sem.at[index], inc=1, device_id=along_z(hop), device_id_type=MESH)
+
+    def told(index):
+        if ring:
+            pl.semaphore_wait(ring_sem.at[index], 1)
 
     @pl.when(place == last)
     def _():
@@ -169,14 +176,13 @@
         lbuf[pl.ds(2 * BLOCK, BLOCK), :] = jnp.zeros((BLOCK, LANES), F32)
         s1_in[...] = jnp.zeros_like(s1_in)
 
-    for hop in (2, 3):
-        @pl.when(place > last - hop)
-        def _():
-            ss_in[hop - 2] = jnp.zeros(ss_in.shape[1:], BF16)
-
-        @pl.when(place < hop)
-        def _():
-            t_in[hop - 2] = jnp.zeros(t_in.shape[1:], BF16)
+    @pl.when(place != 0)
+    def _():
+        ss_in[...] = jnp.zeros_like(ss_in)
+
+    @pl.when(place != last)
+    def _():
+        t_in[...] = jnp.zeros_like(t_in)
 
     @pl.when(place == 0)
     def _():
@@ -225,7 +231,10 @@
     for load in loads[3:]:
         load.wait()
     pl.semaphore_wait(barrier, partners)
-    send(L_UP, TOT1, TOT2, TOT3, Q_UP, G_UP)
+    send(L_UP, TOT1, TOT2, TOT3)
+    send(Q_UP, G_UP, places=place < last)
+    tell(0, 1)
+    tell(1, z_size - 1)
 
     def beside(a):
         parts = [part[:, :32] for part in pieces(a, 3)]
@@ -313,7 +322,10 @@
         return carry
 
     each_pair(own_step)
-    send(S_UP, SS2_UP, SS3_UP, P_DN)
+    send(SS1_UP, SS2_UP, SS3_UP)
+    send(Q_UP, G_UP, places=place == last)
+    send(S_UP, places=place != 2)
+    send(P_DN, places=place != 1)
 
     block_rows(log_own, 0, 0)
     block_rows(log_own, 1, BLOCK)
@@ -398,7 +410,31 @@
     each_pair(next_step)
     send(T2_DN, T3_DN, R_DN)
 
+    told(0)
+    told(1)
+    tell(2, 1)
+    tell(3, z_size - 1)
     each_pair(window_step, 3, PAIRS)
+    told(2)
+    told(3)
+    tell(4, 1)
+    own0 = jnp.exp(lx[BLOCK - 1 : BLOCK, :])
+    own1 = jnp.exp(lx[LANES - 1 : LANES, :])
+
+    @pl.when(place == 2)
+    def _():
+        messages[SS1_UP][0].wait_recv()
+        s1_out[...] = (s1c[...] + own1 * ss_held[...].astype(F32)).astype(BF16)
+        messages[S_UP][0].start()
+
+    @pl.when(place == 1)
+    def _():
+        messages[P_DN][0].wait_recv()
+        messages[R_DN][0].wait_recv()
+        entered = own0 * p_in[...].astype(F32) + r_in[...].astype(F32)
+        p_out[...] = (c1c[...] + own1 * entered).astype(BF16)
+        messages[P_DN][0].start()
+
     block_rows(lbuf[pl.ds(BLOCK, LANES), :], 2, BLOCK)
 
     received(Q_UP, G_UP)
@@ -440,8 +476,6 @@
     prev1_fall1 = jnp.exp(falls[2][1:2])
     prev1_all = jnp.exp(falls[2][0:1] + falls[2][1:2])
     prev2_fall1 = jnp.exp(falls[1][1:2])
-    own0 = jnp.exp(lx[BLOCK - 1 : BLOCK, :])
-    own1 = jnp.exp(lx[LANES - 1 : LANES, :])
     next0 = jnp.exp(lx[3 * BLOCK - 1 :, :])
     z_grad = s1_in[...].astype(F32) + next1_fall1 * (
         ss_in[0].astype(F32) + next2_all * ss_in[1].astype(F32)
@@ -509,7 +543,8 @@
     )
     d_decay1 = decay_grad(1) + twice(lower, entered * tail1)
 
-    received(P_DN, R_DN, T2_DN, T3_DN)
+    received(P_DN, R_DN, places=place != 1)
+    received(T2_DN, T3_DN)
     memory = (
         p_in[...].astype(F32)
         + prev1_fall1 * t_in[0].astype(F32)
@@ -639,6 +674,7 @@
         one.wait_recv()
     made += more
     third[z] = added(second, y_size)
+    told(4)
     more = exchange(8 + y_size, z_size, along_z, lambda hop: third.at[z], third.at[z])
     for one in more:
         one.wait_recv()
@@ -672,7 +708,7 @@
         (gate.shape, F32), (coef.shape, F32), (rate.shape, F32),
         (full, BF16), (full, BF16), (full, BF16), (full, BF16),
         (block, BF16), (block, BF16), ((3 * BLOCK, LANES), F32), ((8, LANES), F32), ((3, 8, LANES), F32),
-        (block, BF16), (block, BF16), (block, BF16), ((2,) + block, BF16),
+        (block, BF16), (block, BF16), (block, BF16), (block, BF16), ((2,) + block, BF16),
         (block, BF16), (block, BF16), (block, BF16), (block, BF16), (block, BF16), ((2,) + block, BF16),
         (block, BF16), (block, BF16), ((BLOCK, LANES), F32), ((BLOCK, LANES), F32),
         ((8, WIDTH), F32), ((3 * BLOCK, WIDTH), F32), (full, F32), ((4 * BLOCK, WIDTH), F32),
@@ -694,7 +730,8 @@
         + [
             pltpu.SemaphoreType.DMA((number,))
             for number in (LOADS, STORES, MESSAGES, MESSAGES, count, count)
-        ],
+        ]
+        + [pltpu.SemaphoreType.REGULAR((5,))],
         compiler_params=pltpu.CompilerParams(
             collective_id=0, has_side_effects=True, vmem_limit_bytes=56 * 2**20
         ),

time: 47.7 us -> 47.7 us (level)
  no operation moved by 1% of the time
where the time goes in v4:
time: 47.7 us; the launch traced here: 47.6 us
  Pallas kernels  46.9 us (98%)
  between operations  0.64 us (1%)
    pallas_call x1, Pallas kernels, main_call(): pl.pallas_call(functools.partial(main_kernel, z_size, y_size), out_shape=...  44.9 us
    pallas_call x1, Pallas kernels, hand_out(): pl.pallas_call(hand_out_kernel, out_shape=shapes[:4] + params, in_specs=[...  2.08 us

profile of v4, /device:TPU:1, one launch (start us, length us, event | category | flops | bytes accessed | tf_op | source)
XLA Modules:
  0.0 47.6 jit_solution(10246688133912007440)
XLA Ops:
  0.6 44.9 %window_backward.1 = (bf16[128,1024]{1,0:T(8,128)(2,1)}, bf16[128,1024]{1,0:T(8,128)(2,1)}, bf16[128,1024]{1,0:T(8,128)(2,1)}, bf16[128,1024]{1,0:T(8,128)(2,1)}, bf16[8,48,128]{2,1,0:T(8,128)(2,1)}) custom-call(bf16[128,1024]{1,0:T(8,128)(2,1)} %bitcast.15, bf16[128,1024]{1,0:T(8,128)(2,1)} %bitcast.16, bf16[128,1024]{1,0:T(8,128)(2,1)} %bitcast.17, ...), custom_call_target="tpu_custom_call" | custom-call | tf_op jit(solution)/shard_map/window_backward/pallas_call | solution.py:724
  45.5 2.1 %hand_out.1 = (bf16[128,1024]{1,0:T(8,128)(2,1)}, bf16[128,1024]{1,0:T(8,128)(2,1)}, bf16[128,1024]{1,0:T(8,128)(2,1)}, bf16[128,1024]{1,0:T(8,128)(2,1)}, f32[3...) custom-call(bf16[128,1024]{1,0:T(8,128)(2,1)} %get-tuple-element.19.refs_0_, ...), custom_call_target="tpu_custom_call" | custom-call | tf_op jit(solution)/shard_map/hand_out/pallas_call | solution.py:777

commit v5 on v4

--- a/solution.py
+++ b/solution.py
@@ -53,6 +53,8 @@
 STORES = 5
 TALL = 48
 NEVER = -1e30
+WIDE = 8
+GROUP = 4
 
 
 def main_kernel(
@@ -64,7 +66,7 @@
     qn, gn, lbuf, tot, tot_in, s1_out, ss_out, s1_in, ss_held, ss_in, p_out, r_out, t_out, p_in, r_in, t_in,
     dqn_out, dqn_in, dan_out, dan_in,
     lrow, lx, gamma_x, blast_x, qf, wk, gq, s1c, u0c, c1c, m_in, m_mid, n_mid, n_end, z_end,
-    dqf, dwk, dvf, gmat, xmat, coef_sum,
+    dqf, dwk, dvf, gmat, xmat, coef_sum, keys_held, values_held,
     mine, first, second, third, done,
     load_sem, store_sem, send_sem, recv_sem, sum_send, sum_recv, ring_sem,
 ):
@@ -276,6 +278,16 @@
     def each_pair(step, begin=0, end=PAIRS):
         lax.fori_loop(begin, end, step, 0, unroll=end - begin)
 
+    def together(step, group=GROUP):
+        def several(index, carry):
+            step([index * group + offset for offset in range(group)])
+            return carry
+
+        return several
+
+    def all_pairs(step, group=WIDE):
+        each_pair(together(step, group), 0, PAIRS // group)
+
     def lanes_of(pair):
         return pl.ds(pl.multiple_of(pair * LANES, LANES), LANES)
 
@@ -293,35 +305,39 @@
     def weighted(a, weights):
         return (a.astype(F32) * weights).astype(BF16)
 
-    def own_step(pair, carry):
-        at = lanes_of(pair)
-        coef = coef_ref[:, at]
-        q_feat = phi(q_ref[:, at], coef).astype(BF16)
-        qf[pl.ds(0, LANES), at] = q_feat
-        keys = (phi(k_ref[:, at], coef) * gamma_x[:, at]).astype(BF16)
-        wk[:, at] = keys
-        logs = lx[pl.ds(0, LANES), at]
-        scaled = weighted(g_ref[:, at], jnp.exp(logs))
-        gq[:, at] = scaled
-        s0 = compact(tn(q_feat[:BLOCK], scaled[:BLOCK]))
-        s1 = compact(tn(q_feat[BLOCK:], scaled[BLOCK:]))
-        fall0 = jnp.exp(logs[BLOCK - 1 : BLOCK])
-        fall1 = jnp.exp(logs[LANES - 1 :])
-        s1_out[:, at] = s1.astype(BF16)
-        ss_out[:, at] = (s0 + fall0 * s1).astype(BF16)
-        values = v_ref[:, at]
-        weights = blast_x[pl.ds(0, 3 * BLOCK), at]
-        carried0 = weighted(keys[:BLOCK], weights[:BLOCK])
-        carried1 = weighted(keys, weights[BLOCK:])
-        u0 = compact(tn(carried0, values[:BLOCK]))
-        c1 = fall1 * u0 + compact(tn(carried1, values))
-        u0c[:, at] = u0
-        c1c[:, at] = c1
-        s1c[:, at] = s1
-        p_out[:, at] = c1.astype(BF16)
-        return carry
-
-    each_pair(own_step)
+    def own_step(pairs):
+        ats = [lanes_of(pair) for pair in pairs]
+        coefs = [coef_ref[:, at] for at in ats]
+        q_feat = [phi(q_ref[:, at], coef).astype(BF16) for at, coef in zip(ats, coefs)]
+        keys = [
+            (phi(k_ref[:, at], coef) * gamma_x[:, at]).astype(BF16) for at, coef in zip(ats, coefs)
+        ]
+        logs = [lx[pl.ds(0, LANES), at] for at in ats]
+        scaled = [weighted(g_ref[:, at], jnp.exp(a)) for at, a in zip(ats, logs)]
+        values = [v_ref[:, at] for at in ats]
+        carried0 = [
+            weighted(a[:BLOCK], blast_x[pl.ds(0, BLOCK), at]) for at, a in zip(ats, keys)
+        ]
+        carried1 = [weighted(a, blast_x[pl.ds(BLOCK, LANES), at]) for at, a in zip(ats, keys)]
+        s0 = [compact(tn(a[:BLOCK], b[:BLOCK])) for a, b in zip(q_feat, scaled)]
+        s1 = [compact(tn(a[BLOCK:], b[BLOCK:])) for a, b in zip(q_feat, scaled)]
+        u0 = [compact(tn(a, b[:BLOCK])) for a, b in zip(carried0, values)]
+        c1 = [compact(tn(a, b)) for a, b in zip(carried1, values)]
+        for index, at in enumerate(ats):
+            qf[pl.ds(0, LANES), at] = q_feat[index]
+            wk[:, at] = keys[index]
+            gq[:, at] = scaled[index]
+            fall0 = jnp.exp(logs[index][BLOCK - 1 : BLOCK])
+            fall1 = jnp.exp(logs[index][LANES - 1 :])
+            s1_out[:, at] = s1[index].astype(BF16)
+            ss_out[:, at] = (s0[index] + fall0 * s1[index]).astype(BF16)
+            end = fall1 * u0[index] + c1[index]
+            u0c[:, at] = u0[index]
+            c1c[:, at] = end
+            s1c[:, at] = s1[index]
+            p_out[:, at] = end.astype(BF16)
+
+    all_pairs(own_step)
     send(SS1_UP, SS2_UP, SS3_UP)
     send(Q_UP, G_UP, places=place == last)
     send(S_UP, places=place != 2)
@@ -341,55 +357,82 @@
 
     first_rows, last_rows = slice(0, BLOCK), slice(BLOCK, LANES)
 
-    def tile(keys_bd, values_bd, queries, grads, kernel):
-        scores = nt(queries, keys_bd)
-        d_weights = nt(grads, values_bd)
-        weights = (scores * kernel).astype(BF16)
-        d_scores = (d_weights * kernel).astype(BF16)
-        d_kernel = (d_weights * scores).astype(BF16)
+    corner = iota((LANES, LANES), 0) < BLOCK, iota((LANES, LANES), 1) < BLOCK
+    first_head, second_head = corner[0] & corner[1], ~corner[0] & ~corner[1]
+
+    def turned_diagonals(rows):
+        turned = rows.T
+        swapped = jnp.concatenate([turned[:, BLOCK:], turned[:, :BLOCK]], axis=1)
+        none = jnp.zeros_like(turned)
         return (
-            nn(d_scores, keys_bd),
-            compact(tn(weights, grads)),
-            compact(tn(d_scores, queries)),
-            d_kernel,
-        )
-
-    def window_step(pair, carry):
-        at = lanes_of(pair)
-        keys, values = wk[:, at], v_ref[:, at]
-        queries, grads = qf[pl.ds(0, LANES), at], g_ref[:, at]
-        rows = jnp.concatenate(
-            [jnp.broadcast_to(lrow[b : b + 1, at], (BLOCK, LANES)) for b in range(2)], axis=0
-        )
-        decays = jnp.exp(jnp.where(causal, lx[pl.ds(0, LANES), at] - rows, NEVER))
-        low = decays.astype(BF16)
-        start = nn(low[:BLOCK], cur_mask)
-        middle = nn(low[BLOCK:], both_mask)
-        dq0, dv0, dk0, db0 = tile(
-            diagonal(keys[:BLOCK]), diagonal(values[:BLOCK]), queries, grads,
-            jnp.concatenate([start, middle[:, LANES:]], axis=0),
-        )
-        dq1, dv1, dk1, db1 = tile(
-            diagonal(keys[BLOCK:]), diagonal(values[BLOCK:]), queries[BLOCK:], grads[BLOCK:],
-            middle[:, :LANES],
-        )
-        dvf[pl.ds(0, BLOCK), at] = dv0
-        dvf[pl.ds(BLOCK, BLOCK), at] = dv1
-        dwk[pl.ds(0, BLOCK), at] = dk0
-        dwk[pl.ds(BLOCK, BLOCK), at] = dk1
-        dqf[pl.ds(0, BLOCK), at] = dq0[:BLOCK]
-        dqf[pl.ds(BLOCK, BLOCK), at] = dq0[BLOCK:] + dq1
-        d_decays = jnp.concatenate(
-            [
-                nt(db0[:BLOCK], cur_mask),
-                nt(jnp.concatenate([db1, db0[BLOCK:]], axis=1), both_mask),
-            ],
-            axis=0,
-        )
-        gmat[pl.ds(0, LANES), at] = (d_decays * decays).astype(BF16)
-        return carry
-
-    each_pair(window_step, 0, 3)
+            jnp.where(first_head, turned, jnp.where(second_head, swapped, none)),
+            jnp.where(first_head, swapped, jnp.where(second_head, turned, none)),
+        )
+
+    def tiles(keys_bd, keys_t, values_t, queries, grads, kernels):
+        scores = [nn(a, b) for a, b in zip(queries, keys_t)]
+        d_weights = [nn(a, b) for a, b in zip(grads, values_t)]
+        weights = [(a * b).astype(BF16) for a, b in zip(scores, kernels)]
+        d_scores = [(a * b).astype(BF16) for a, b in zip(d_weights, kernels)]
+        d_kernels = [(a * b).astype(BF16) for a, b in zip(d_weights, scores)]
+        d_queries = [nn(a, b) for a, b in zip(d_scores, keys_bd)]
+        d_values = [compact(tn(a, b)) for a, b in zip(weights, grads)]
+        d_keys = [compact(tn(a, b)) for a, b in zip(d_scores, queries)]
+        return d_queries, d_values, d_keys, d_kernels
+
+    def window_step(pairs):
+        ats = [lanes_of(pair) for pair in pairs]
+        keys = [wk[:, at] for at in ats]
+        values = [v_ref[:, at] for at in ats]
+        queries = [qf[pl.ds(0, LANES), at] for at in ats]
+        grads = [g_ref[:, at] for at in ats]
+        rows = [
+            jnp.concatenate(
+                [jnp.broadcast_to(lrow[b : b + 1, at], (BLOCK, LANES)) for b in range(2)], axis=0
+            )
+            for at in ats
+        ]
+        decays = [
+            jnp.exp(jnp.where(causal, lx[pl.ds(0, LANES), at] - row, NEVER))
+            for at, row in zip(ats, rows)
+        ]
+        low = [a.astype(BF16) for a in decays]
+        start = [nn(a[:BLOCK], cur_mask) for a in low]
+        middle = [nn(a[BLOCK:], both_mask) for a in low]
+        keys_t = [turned_diagonals(a) for a in keys]
+        values_t = [turned_diagonals(a) for a in values]
+        for pair, a, b in zip(pairs, keys_t, values_t):
+            keys_held[pair] = a[1]
+            values_held[pair] = b[1]
+        dq0, dv0, dk0, db0 = tiles(
+            [diagonal(a[:BLOCK]) for a in keys], [a[0] for a in keys_t], [a[0] for a in values_t],
+            queries, grads,
+            [jnp.concatenate([a, b[:, LANES:]], axis=0) for a, b in zip(start, middle)],
+        )
+        dq1, dv1, dk1, db1 = tiles(
+            [diagonal(a[BLOCK:]) for a in keys], [a[1] for a in keys_t], [a[1] for a in values_t],
+            [a[BLOCK:] for a in queries], [a[BLOCK:] for a in grads], [a[:, :LANES] for a in middle],
+        )
+        d_decays = [
+            jnp.concatenate(
+                [
+                    nt(a[:BLOCK], cur_mask),
+                    nt(jnp.concatenate([b, a[BLOCK:]], axis=1), both_mask),
+                ],
+                axis=0,
+            )
+            for a, b in zip(db0, db1)
+        ]
+        for index, at in enumerate(ats):
+            dvf[pl.ds(0, BLOCK), at] = dv0[index]
+            dvf[pl.ds(BLOCK, BLOCK), at] = dv1[index]
+            dwk[pl.ds(0, BLOCK), at] = dk0[index]
+            dwk[pl.ds(BLOCK, BLOCK), at] = dk1[index]
+            dqf[pl.ds(0, BLOCK), at] = dq0[index][:BLOCK]
+            dqf[pl.ds(BLOCK, BLOCK), at] = dq0[index][BLOCK:] + dq1[index]
+            gmat[pl.ds(0, LANES), at] = (d_decays[index] * decays[index]).astype(BF16)
+
+    each_pair(together(window_step), 0, PAIRS // GROUP // 2)
 
     received(L_UP)
     log_next = lbuf[pl.ds(2 * BLOCK, BLOCK), :]
@@ -398,23 +441,27 @@
     lx[pl.ds(LANES, BLOCK), :] = expanded[:BLOCK]
     blast_x[pl.ds(3 * BLOCK, BLOCK), :] = expanded[BLOCK:]
 
-    def next_step(pair, carry):
-        at = lanes_of(pair)
-        fall2 = jnp.exp(lx[3 * BLOCK - 1 : 3 * BLOCK, at])
-        carried = weighted(wk[pl.ds(BLOCK, BLOCK), at], blast_x[pl.ds(3 * BLOCK, BLOCK), at])
-        r = compact(tn(carried, v_ref[pl.ds(BLOCK, BLOCK), at]))
-        r_out[:, at] = r.astype(BF16)
-        t_out[:, at] = (fall2 * c1c[:, at] + r).astype(BF16)
-        return carry
-
-    each_pair(next_step)
+    def next_step(pairs):
+        ats = [lanes_of(pair) for pair in pairs]
+        carried = [
+            weighted(wk[pl.ds(BLOCK, BLOCK), at], blast_x[pl.ds(3 * BLOCK, BLOCK), at]) for at in ats
+        ]
+        entering = [
+            compact(tn(a, v_ref[pl.ds(BLOCK, BLOCK), at])) for a, at in zip(carried, ats)
+        ]
+        for r, at in zip(entering, ats):
+            fall2 = jnp.exp(lx[3 * BLOCK - 1 : 3 * BLOCK, at])
+            r_out[:, at] = r.astype(BF16)
+            t_out[:, at] = (fall2 * c1c[:, at] + r).astype(BF16)
+
+    all_pairs(next_step)
     send(T2_DN, T3_DN, R_DN)
 
     told(0)
     told(1)
     tell(2, 1)
     tell(3, z_size - 1)
-    each_pair(window_step, 3, PAIRS)
+    each_pair(together(window_step), PAIRS // GROUP // 2, PAIRS // GROUP)
     told(2)
     told(3)
     tell(4, 1)
@@ -439,27 +486,35 @@
 
     received(Q_UP, G_UP)
 
-    def cross_step(pair, carry):
-        at = lanes_of(pair)
-        queries = phi(qn[:, at], coef_ref[:, at]).astype(BF16)
-        grads = gn[:, at]
-        logs = lx[pl.ds(LANES, BLOCK), at]
-        held = causal[:BLOCK]
-        decays = jnp.exp(jnp.where(held, logs - lrow[2:3, at], NEVER))
-        dq, dv, dk, db = tile(
-            diagonal(wk[pl.ds(BLOCK, BLOCK), at]), diagonal(v_ref[pl.ds(BLOCK, BLOCK), at]),
-            queries, grads, nn(decays.astype(BF16), prev_mask),
-        )
-        dqn_out[:, at] = dq.astype(BF16)
-        raw = qn[:, at].astype(F32)
-        coef_sum[1:2, at] = jnp.sum(dq * (0.125 * raw * raw), axis=0, keepdims=True)
-        dvf[pl.ds(BLOCK, BLOCK), at] = dvf[pl.ds(BLOCK, BLOCK), at] + dv
-        dwk[pl.ds(BLOCK, BLOCK), at] = dwk[pl.ds(BLOCK, BLOCK), at] + dk
-        gmat[pl.ds(LANES, BLOCK), at] = (nt(db, prev_mask) * decays).astype(BF16)
-        c1c[:, at] = compact(tn(queries, weighted(grads, jnp.exp(logs))))
-        return carry
-
-    each_pair(cross_step)
+    def cross_step(pairs):
+        ats = [lanes_of(pair) for pair in pairs]
+        queries = [phi(qn[:, at], coef_ref[:, at]).astype(BF16) for at in ats]
+        grads = [gn[:, at] for at in ats]
+        logs = [lx[pl.ds(LANES, BLOCK), at] for at in ats]
+        decays = [
+            jnp.exp(jnp.where(causal[:BLOCK], a - lrow[2:3, at], NEVER)) for at, a in zip(ats, logs)
+        ]
+        d_queries, d_values, d_keys, d_kernels = tiles(
+            [diagonal(wk[pl.ds(BLOCK, BLOCK), at]) for at in ats],
+            [keys_held[pair] for pair in pairs], [values_held[pair] for pair in pairs],
+            queries, grads, [nn(a.astype(BF16), prev_mask) for a in decays],
+        )
+        entering = [
+            compact(tn(a, weighted(b, jnp.exp(c)))) for a, b, c in zip(queries, grads, logs)
+        ]
+        d_decays = [nt(a, prev_mask) for a in d_kernels]
+        for index, at in enumerate(ats):
+            dqn_out[:, at] = d_queries[index].astype(BF16)
+            raw = qn[:, at].astype(F32)
+            coef_sum[1:2, at] = jnp.sum(
+                d_queries[index] * (0.125 * raw * raw), axis=0, keepdims=True
+            )
+            dvf[pl.ds(BLOCK, BLOCK), at] = dvf[pl.ds(BLOCK, BLOCK), at] + d_values[index]
+            dwk[pl.ds(BLOCK, BLOCK), at] = dwk[pl.ds(BLOCK, BLOCK), at] + d_keys[index]
+            gmat[pl.ds(LANES, BLOCK), at] = (d_decays[index] * decays[index]).astype(BF16)
+            c1c[:, at] = entering[index]
+
+    each_pair(together(cross_step), 0, PAIRS // GROUP)
     send(DQ_DN)
 
     def decay_grad(block):
@@ -492,46 +547,57 @@
         xmat[pl.ds(index * BLOCK, BLOCK), at] = (d_role * own_keys).astype(BF16)
         return (own_keys * weights).astype(BF16), d_role * weights
 
-    def outer_step(pair, carry):
-        at = lanes_of(pair)
+    def outer_step(pairs):
+        ats = [lanes_of(pair) for pair in pairs]
         rows = pl.ds(BLOCK, BLOCK)
-        grads = diagonal(z_end[:, at])
-        carried, d_keys = enter(3, wk[rows, at], nt(v_ref[rows, at], grads), at)
-        dwk[rows, at] = dwk[rows, at] + d_keys
-        dvf[rows, at] = dvf[rows, at] + nn(carried, grads)
-        return carry
-
-    each_pair(outer_step)
+        grads = [diagonal(z_end[:, at]) for at in ats]
+        d_roles = [nt(v_ref[rows, at], a) for at, a in zip(ats, grads)]
+        entered = [enter(3, wk[rows, at], a, at) for at, a in zip(ats, d_roles)]
+        d_values = [nn(a[0], b) for a, b in zip(entered, grads)]
+        for at, a, b in zip(ats, entered, d_values):
+            dwk[rows, at] = dwk[rows, at] + a[1]
+            dvf[rows, at] = dvf[rows, at] + b
+
+    all_pairs(outer_step)
     d_last = nt(xmat[pl.ds(3 * BLOCK, BLOCK), :], spread)
     dan_out[...] = decay_grad(2) + twice(lower, twice(after, d_last) * tail2)
     send(DA_DN)
 
-    def inner_step(pair, carry):
-        at = lanes_of(pair)
-        keys, values = wk[:, at], v_ref[:, at]
-        grads_end = diagonal(n_end[:, at])
-        both = jnp.concatenate([diagonal(n_mid[:, at]), grads_end], axis=0)
-        d_first = nt(values[:BLOCK], both)
-        carried0, d_keys0 = enter(0, keys[:BLOCK], d_first[:, :LANES], at)
-        carried1, d_keys1 = enter(1, keys[:BLOCK], d_first[:, LANES:], at)
-        carried2, d_keys2 = enter(2, keys[BLOCK:], nt(values[BLOCK:], grads_end), at)
-        dv_ref[pl.ds(0, BLOCK), at] = (
-            dvf[pl.ds(0, BLOCK), at] + nn(jnp.concatenate([carried0, carried1], axis=1), both)
-        ).astype(BF16)
-        dv_ref[pl.ds(BLOCK, BLOCK), at] = (
-            dvf[pl.ds(BLOCK, BLOCK), at] + nn(carried2, grads_end)
-        ).astype(BF16)
-        d_keys = dwk[:, at] + jnp.concatenate([d_keys0 + d_keys1, d_keys2], axis=0)
-        coef = coef_ref[:, at]
-        raw = k_ref[:, at].astype(F32)
-        d_feat = d_keys * gamma_x[:, at]
-        square = 0.125 * raw * raw
-        xmat[pl.ds(6 * BLOCK, LANES), at] = (d_keys * (0.125 * raw + coef * square)).astype(BF16)
-        dk_ref[:, at] = (d_feat * (0.125 + (0.25 * coef) * raw)).astype(BF16)
-        coef_sum[0:1, at] = jnp.sum(d_feat * square, axis=0, keepdims=True)
-        return carry
-
-    each_pair(inner_step)
+    def inner_step(pairs):
+        ats = [lanes_of(pair) for pair in pairs]
+        keys = [wk[:, at] for at in ats]
+        values = [v_ref[:, at] for at in ats]
+        ends = [diagonal(n_end[:, at]) for at in ats]
+        both = [
+            jnp.concatenate([diagonal(n_mid[:, at]), a], axis=0) for at, a in zip(ats, ends)
+        ]
+        d_first = [nt(a[:BLOCK], b) for a, b in zip(values, both)]
+        d_second = [nt(a[BLOCK:], b) for a, b in zip(values, ends)]
+        enter0 = [enter(0, a[:BLOCK], b[:, :LANES], at) for a, b, at in zip(keys, d_first, ats)]
+        enter1 = [enter(1, a[:BLOCK], b[:, LANES:], at) for a, b, at in zip(keys, d_first, ats)]
+        enter2 = [enter(2, a[BLOCK:], b, at) for a, b, at in zip(keys, d_second, ats)]
+        dv0 = [
+            nn(jnp.concatenate([a[0], b[0]], axis=1), c) for a, b, c in zip(enter0, enter1, both)
+        ]
+        dv1 = [nn(a[0], b) for a, b in zip(enter2, ends)]
+        for index, at in enumerate(ats):
+            dv_ref[:, at] = (
+                dvf[:, at] + jnp.concatenate([dv0[index], dv1[index]], axis=0)
+            ).astype(BF16)
+            d_keys = dwk[:, at] + jnp.concatenate(
+                [enter0[index][1] + enter1[index][1], enter2[index][1]], axis=0
+            )
+            coef = coef_ref[:, at]
+            raw = k_ref[:, at].astype(F32)
+            d_feat = d_keys * gamma_x[:, at]
+            square = 0.125 * raw * raw
+            xmat[pl.ds(6 * BLOCK, LANES), at] = (
+                d_keys * (0.125 * raw + coef * square)
+            ).astype(BF16)
+            dk_ref[:, at] = (d_feat * (0.125 + (0.25 * coef) * raw)).astype(BF16)
+            coef_sum[0:1, at] = jnp.sum(d_feat * square, axis=0, keepdims=True)
+
+    all_pairs(inner_step)
     stores[1].start()
     stores[2].start()
     d_enter = nt(xmat[pl.ds(0, 3 * BLOCK), :], spread)
@@ -563,30 +629,33 @@
     )
     fall_grad = sum(nt(part, spread) for part in pieces(fall_grad, 2))
 
-    def query_step(pair, carry):
-        at = lanes_of(pair)
-        scaled = gq[:, at]
-        carried = jnp.concatenate(
-            [
-                nt(scaled[:BLOCK], diagonal(m_in[:, at])),
-                nt(scaled[BLOCK:], diagonal(m_mid[:, at])),
-            ],
-            axis=0,
-        )
-        xmat[pl.ds(4 * BLOCK, LANES), at] = (
-            carried * qf[pl.ds(0, LANES), at].astype(F32)
-        ).astype(BF16)
-        raw = q_ref[:, at].astype(F32)
-        d_feat = dqf[:, at] + carried
-        dqf[:, at] = d_feat
-        coef_sum[0:1, at] = (
-            coef_sum[0:1, at]
-            + coef_sum[1:2, at]
-            + jnp.sum(d_feat * (0.125 * raw * raw), axis=0, keepdims=True)
-        )
-        return carry
-
-    each_pair(query_step)
+    def query_step(pairs):
+        ats = [lanes_of(pair) for pair in pairs]
+        scaled = [gq[:, at] for at in ats]
+        carried = [
+            jnp.concatenate(
+                [
+                    nt(a[:BLOCK], diagonal(m_in[:, at])),
+                    nt(a[BLOCK:], diagonal(m_mid[:, at])),
+                ],
+                axis=0,
+            )
+            for a, at in zip(scaled, ats)
+        ]
+        for a, at in zip(carried, ats):
+            xmat[pl.ds(4 * BLOCK, LANES), at] = (
+                a * qf[pl.ds(0, LANES), at].astype(F32)
+            ).astype(BF16)
+            raw = q_ref[:, at].astype(F32)
+            d_feat = dqf[:, at] + a
+            dqf[:, at] = d_feat
+            coef_sum[0:1, at] = (
+                coef_sum[0:1, at]
+                + coef_sum[1:2, at]
+                + jnp.sum(d_feat * (0.125 * raw * raw), axis=0, keepdims=True)
+            )
+
+    all_pairs(query_step)
     d_out = nt(xmat[pl.ds(4 * BLOCK, LANES), :], spread)
     received(DA_DN)
     d_decay = jnp.concatenate(
@@ -717,6 +786,7 @@
         (block, BF16), (block, BF16), (block, BF16), (block, BF16), (block, BF16),
         (full, F32), (full, F32), (full, F32),
         ((3 * BLOCK, WIDTH), BF16), ((8 * BLOCK, WIDTH), BF16), ((8, WIDTH), F32),
+        ((PAIRS, LANES, LANES), BF16), ((PAIRS, LANES, LANES), BF16),
         ((8,) + tile, BF16), ((8,) + tile, BF16), ((y_size,) + tile, BF16), ((z_size,) + tile, BF16),
         (tile, BF16),
     ]

time: 47.7 us -> 47.2 us (0.990)
  Pallas kernels: 46.9 us -> 46.4 us
    pallas_call x1, Pallas kernels: 44.9 us -> 44.4 us  [main_call(): pl.pallas_call(functools.partial(main_kernel, z_size, y_size), out_shape=...]
where the time goes in v5:
time: 47.2 us; the launch traced here: 47.1 us
  Pallas kernels  46.4 us (98%)
  between operations  0.64 us (1%)
    pallas_call x1, Pallas kernels, main_call(): pl.pallas_call(functools.partial(main_kernel, z_size, y_size), out_shape=...  44.4 us
    pallas_call x1, Pallas kernels, hand_out(): pl.pallas_call(hand_out_kernel, out_shape=shapes[:4] + params, in_specs=[...  2.08 us

profile of v5, /device:TPU:1, one launch (start us, length us, event | category | flops | bytes accessed | tf_op | source)
XLA Modules:
  0.0 47.1 jit_solution(8858455421207688643)
XLA Ops:
  0.6 44.4 %window_backward.1 = (bf16[128,1024]{1,0:T(8,128)(2,1)}, bf16[128,1024]{1,0:T(8,128)(2,1)}, bf16[128,1024]{1,0:T(8,128)(2,1)}, bf16[128,1024]{1,0:T(8,128)(2,1)}, bf16[8,48,128]{2,1,0:T(8,128)(2,1)}) custom-call(bf16[128,1024]{1,0:T(8,128)(2,1)} %bitcast.15, bf16[128,1024]{1,0:T(8,128)(2,1)} %bitcast.16, bf16[128,1024]{1,0:T(8,128)(2,1)} %bitcast.17, ...), custom_call_target="tpu_custom_call" | custom-call | tf_op jit(solution)/shard_map/window_backward/pallas_call | solution.py:794
  45.0 2.1 %hand_out.1 = (bf16[128,1024]{1,0:T(8,128)(2,1)}, bf16[128,1024]{1,0:T(8,128)(2,1)}, bf16[128,1024]{1,0:T(8,128)(2,1)}, bf16[128,1024]{1,0:T(8,128)(2,1)}, f32[3...) custom-call(bf16[128,1024]{1,0:T(8,128)(2,1)} %get-tuple-element.19.refs_0_, ...), custom_call_target="tpu_custom_call" | custom-call | tf_op jit(solution)/shard_map/hand_out/pallas_call | solution.py:847

commit v6 on v5

--- a/solution.py
+++ b/solution.py
@@ -46,9 +46,9 @@
     return lax.broadcasted_iota(jnp.int32, shape, dimension)
 
 
-Q_UP, G_UP, L_UP, S_UP, SS1_UP, SS2_UP, SS3_UP, TOT1, TOT2, TOT3 = range(10)
-P_DN, R_DN, T2_DN, T3_DN, DQ_DN, DA_DN = range(10, 16)
-MESSAGES = 16
+Q_UP, G_UP, L_UP, S_UP, SS_ROUND, SS_ON, SS_BACK, SS_UP, TOT1, TOT2, TOT3 = range(11)
+P_DN, R_DN, T2_DN, T3_DN, DQ_DN, DA_DN = range(11, 17)
+MESSAGES = 17
 LOADS = 8
 STORES = 5
 TALL = 48
@@ -102,7 +102,7 @@
             device_id_type=MESH,
         )
 
-    up1, up2, up3 = place - 1, place - 2, place - 3
+    up1, up3 = place - 1, place - 3
     dn1, dn2, dn3 = place + 1, place + 2, place + 3
     around = [lax.rem(place + 4 - hop, 4) for hop in (1, 2, 3)]
     always = place >= 0
@@ -114,9 +114,10 @@
             copy(lbuf.at[pl.ds(0, BLOCK)], lbuf.at[pl.ds(2 * BLOCK, BLOCK)], L_UP, up1), later, earlier
         ),
         S_UP: (copy(s1_out, s1_in, S_UP, up1), later, earlier),
-        SS1_UP: (copy(ss_out, ss_held, SS1_UP, up1), place == 3, place == 2),
-        SS2_UP: (copy(ss_out, ss_in.at[0], SS2_UP, up2), place == 2, place == 0),
-        SS3_UP: (copy(ss_out, ss_in.at[1], SS3_UP, up3), place == 3, place == 0),
+        SS_UP: (copy(ss_out, ss_in.at[1], SS_UP, up3), place == 3, place == 0),
+        SS_ON: (copy(ss_in.at[1], ss_in.at[0], SS_ON, dn1), place == 0, place == 1),
+        SS_ROUND: (copy(ss_out, ss_held, SS_ROUND, dn1), place == 2, place == 3),
+        SS_BACK: (copy(ss_held, ss_in.at[0], SS_BACK, up3), place == 3, place == 0),
         TOT1: (copy(tot, tot_in.at[0], TOT1, around[0]), always, always),
         TOT2: (copy(tot, tot_in.at[1], TOT2, around[1]), always, always),
         TOT3: (copy(tot, tot_in.at[2], TOT3, around[2]), always, always),
@@ -178,9 +179,13 @@
         lbuf[pl.ds(2 * BLOCK, BLOCK), :] = jnp.zeros((BLOCK, LANES), F32)
         s1_in[...] = jnp.zeros_like(s1_in)
 
-    @pl.when(place != 0)
+    @pl.when(place >= 2)
     def _():
-        ss_in[...] = jnp.zeros_like(ss_in)
+        ss_in[0] = jnp.zeros(ss_in.shape[1:], BF16)
+
+    @pl.when(place >= 1)
+    def _():
+        ss_in[1] = jnp.zeros(ss_in.shape[1:], BF16)
 
     @pl.when(place != last)
     def _():
@@ -234,7 +239,7 @@
         load.wait()
     pl.semaphore_wait(barrier, partners)
     send(L_UP, TOT1, TOT2, TOT3)
-    send(Q_UP, G_UP, places=place < last)
+    send(Q_UP, G_UP)
     tell(0, 1)
     tell(1, z_size - 1)
 
@@ -338,9 +343,7 @@
             p_out[:, at] = end.astype(BF16)
 
     all_pairs(own_step)
-    send(SS1_UP, SS2_UP, SS3_UP)
-    send(Q_UP, G_UP, places=place == last)
-    send(S_UP, places=place != 2)
+    send(SS_UP, SS_ROUND, S_UP)
     send(P_DN, places=place != 1)
 
     block_rows(log_own, 0, 0)
@@ -468,11 +471,15 @@
     own0 = jnp.exp(lx[BLOCK - 1 : BLOCK, :])
     own1 = jnp.exp(lx[LANES - 1 : LANES, :])
 
-    @pl.when(place == 2)
+    @pl.when(place == 0)
     def _():
-        messages[SS1_UP][0].wait_recv()
-        s1_out[...] = (s1c[...] + own1 * ss_held[...].astype(F32)).astype(BF16)
-        messages[S_UP][0].start()
+        messages[SS_UP][0].wait_recv()
+        messages[SS_ON][0].start()
+
+    @pl.when(place == last)
+    def _():
+        messages[SS_ROUND][0].wait_recv()
+        messages[SS_BACK][0].start()
 
     @pl.when(place == 1)
     def _():
@@ -517,13 +524,18 @@
     each_pair(together(cross_step), 0, PAIRS // GROUP)
     send(DQ_DN)
 
-    def decay_grad(block):
-        later = nn(upper_in, gmat[pl.ds(block * BLOCK, BLOCK), :])
-        lanes = iota((BLOCK, WIDTH), 1) % BLOCK
-        kept = jnp.where(lanes < iota((BLOCK, WIDTH), 0), later, 0.0)
-        return nt(kept.astype(BF16), spread)
-
-    received(TOT1, S_UP, TOT2, SS2_UP, SS3_UP, TOT3)
+    upper_both = flag(same & (col >= row))
+    later_sums = jnp.concatenate(
+        [
+            nn(upper_both, gmat[pl.ds(0, LANES), :]),
+            nn(upper_in, gmat[pl.ds(LANES, BLOCK), :]),
+        ],
+        axis=0,
+    )
+    before = (iota((3 * BLOCK, WIDTH), 1) % BLOCK) < (iota((3 * BLOCK, WIDTH), 0) % BLOCK)
+    window_grads = nt(jnp.where(before, later_sums, 0.0).astype(BF16), spread)
+
+    received(TOT1, S_UP, TOT2, SS_ON, SS_BACK, TOT3)
     falls = expand(jnp.concatenate([tot_in[slot] for slot in range(3)], axis=0))
     falls = [falls[8 * slot : 8 * slot + 8] for slot in range(3)]
     next1_fall1 = jnp.exp(falls[0][1:2])
@@ -560,7 +572,7 @@
 
     all_pairs(outer_step)
     d_last = nt(xmat[pl.ds(3 * BLOCK, BLOCK), :], spread)
-    dan_out[...] = decay_grad(2) + twice(lower, twice(after, d_last) * tail2)
+    dan_out[...] = window_grads[LANES:] + twice(lower, twice(after, d_last) * tail2)
     send(DA_DN)
 
     def inner_step(pairs):
@@ -602,12 +614,15 @@
     stores[2].start()
     d_enter = nt(xmat[pl.ds(0, 3 * BLOCK), :], spread)
     d_gamma = nt(xmat[pl.ds(6 * BLOCK, LANES), :], spread_gate)
-    d_decay0 = decay_grad(0) + twice(lower, twice(at_or_before, d_enter[:BLOCK]) * tail0)
-    entered = nn(
+    entered0 = twice(at_or_before, d_enter[:BLOCK])
+    entered1 = nn(
         jnp.concatenate([at_or_before, at_or_before, after, after], axis=1),
         jnp.concatenate(pieces(d_enter[2 * BLOCK :], 2) + pieces(d_enter[BLOCK : 2 * BLOCK], 2), axis=0),
     )
-    d_decay1 = decay_grad(1) + twice(lower, entered * tail1)
+    lower_both = flag(same & (col < row))
+    d_decay = window_grads[:LANES] + twice(
+        lower_both, jnp.concatenate([entered0 * tail0, entered1 * tail1], axis=0)
+    )
 
     received(P_DN, R_DN, places=place != 1)
     received(T2_DN, T3_DN)
@@ -657,11 +672,12 @@
 
     all_pairs(query_step)
     d_out = nt(xmat[pl.ds(4 * BLOCK, LANES), :], spread)
+    d_decay = d_decay + twice(upper_both, d_out)
     received(DA_DN)
-    d_decay = jnp.concatenate(
+    d_decay = d_decay + jnp.concatenate(
         [
-            d_decay0 + dan_in[...] + twice(upper_in, d_out[:BLOCK]) + fall_grad[0:1],
-            d_decay1 + twice(upper_in, d_out[BLOCK:]) + fall_grad[1:2],
+            dan_in[...] + fall_grad[0:1],
+            jnp.broadcast_to(fall_grad[1:2], (BLOCK, LANES)),
         ],
         axis=0,
     )

time: 47.2 us -> 45.3 us (0.960)
  Pallas kernels: 46.4 us -> 44.5 us
    pallas_call x1, Pallas kernels: 44.4 us -> 42.4 us  [main_call(): pl.pallas_call(functools.partial(main_kernel, z_size, y_size), out_shape=...]
where the time goes in v6:
time: 45.3 us; the launch traced here: 45.2 us
  Pallas kernels  44.5 us (98%)
  between operations  0.64 us (1%)
    pallas_call x1, Pallas kernels, main_call(): pl.pallas_call(functools.partial(main_kernel, z_size, y_size), out_shape=...  42.4 us
    pallas_call x1, Pallas kernels, hand_out(): pl.pallas_call(hand_out_kernel, out_shape=shapes[:4] + params, in_specs=[...  2.08 us

profile of v6, /device:TPU:1, one launch (start us, length us, event | category | flops | bytes accessed | tf_op | source)
XLA Modules:
  0.0 45.2 jit_solution(17220176377692491714)
XLA Ops:
  0.6 42.4 %window_backward.1 = (bf16[128,1024]{1,0:T(8,128)(2,1)}, bf16[128,1024]{1,0:T(8,128)(2,1)}, bf16[128,1024]{1,0:T(8,128)(2,1)}, bf16[128,1024]{1,0:T(8,128)(2,1)}, bf16[8,48,128]{2,1,0:T(8,128)(2,1)}) custom-call(bf16[128,1024]{1,0:T(8,128)(2,1)} %bitcast.15, bf16[128,1024]{1,0:T(8,128)(2,1)} %bitcast.16, bf16[128,1024]{1,0:T(8,128)(2,1)} %bitcast.17, ...), custom_call_target="tpu_custom_call" | custom-call | tf_op jit(solution)/shard_map/window_backward/pallas_call | solution.py:810
  43.1 2.1 %hand_out.1 = (bf16[128,1024]{1,0:T(8,128)(2,1)}, bf16[128,1024]{1,0:T(8,128)(2,1)}, bf16[128,1024]{1,0:T(8,128)(2,1)}, bf16[128,1024]{1,0:T(8,128)(2,1)}, f32[3...) custom-call(bf16[128,1024]{1,0:T(8,128)(2,1)} %get-tuple-element.19.refs_0_, ...), custom_call_target="tpu_custom_call" | custom-call | tf_op jit(solution)/shard_map/hand_out/pallas_call | solution.py:863

commit v7 on v6

--- a/solution.py
+++ b/solution.py
@@ -435,7 +435,6 @@
             dqf[pl.ds(BLOCK, BLOCK), at] = dq0[index][BLOCK:] + dq1[index]
             gmat[pl.ds(0, LANES), at] = (d_decays[index] * decays[index]).astype(BF16)
 
-    each_pair(together(window_step), 0, PAIRS // GROUP // 2)
 
     received(L_UP)
     log_next = lbuf[pl.ds(2 * BLOCK, BLOCK), :]
@@ -464,7 +463,7 @@
     told(1)
     tell(2, 1)
     tell(3, z_size - 1)
-    each_pair(together(window_step), PAIRS // GROUP // 2, PAIRS // GROUP)
+    each_pair(together(window_step), 0, PAIRS // GROUP)
     told(2)
     told(3)
     tell(4, 1)

time: 45.3 us -> 45.3 us (level)
  no operation moved by 1% of the time
where the time goes in v7:
time: 45.3 us; the launch traced here: 45.2 us
  Pallas kernels  44.5 us (98%)
  between operations  0.64 us (1%)
    pallas_call x1, Pallas kernels, main_call(): pl.pallas_call(functools.partial(main_kernel, z_size, y_size), out_shape=...  42.4 us
    pallas_call x1, Pallas kernels, hand_out(): pl.pallas_call(hand_out_kernel, out_shape=shapes[:4] + params, in_specs=[...  2.08 us

profile of v7, /device:TPU:1, one launch (start us, length us, event | category | flops | bytes accessed | tf_op | source)
XLA Modules:
  0.0 45.2 jit_solution(4265013589798518368)
XLA Ops:
  0.6 42.4 %window_backward.1 = (bf16[128,1024]{1,0:T(8,128)(2,1)}, bf16[128,1024]{1,0:T(8,128)(2,1)}, bf16[128,1024]{1,0:T(8,128)(2,1)}, bf16[128,1024]{1,0:T(8,128)(2,1)}, bf16[8,48,128]{2,1,0:T(8,128)(2,1)}) custom-call(bf16[128,1024]{1,0:T(8,128)(2,1)} %bitcast.15, bf16[128,1024]{1,0:T(8,128)(2,1)} %bitcast.16, bf16[128,1024]{1,0:T(8,128)(2,1)} %bitcast.17, ...), custom_call_target="tpu_custom_call" | custom-call | tf_op jit(solution)/shard_map/window_backward/pallas_call | solution.py:809
  43.1 2.1 %hand_out.1 = (bf16[128,1024]{1,0:T(8,128)(2,1)}, bf16[128,1024]{1,0:T(8,128)(2,1)}, bf16[128,1024]{1,0:T(8,128)(2,1)}, bf16[128,1024]{1,0:T(8,128)(2,1)}, f32[3...) custom-call(bf16[128,1024]{1,0:T(8,128)(2,1)} %get-tuple-element.19.refs_0_, ...), custom_call_target="tpu_custom_call" | custom-call | tf_op jit(solution)/shard_map/hand_out/pallas_call | solution.py:862
